TPU v7x, 512 devices: a whole 4x8x8 slice. The times are simulated.
512 devices in a mesh: seq: 128 (over z_hi, y, x, core), sub: 4 (over z_lo).
Axes of the slice: x: 4, y: 8, z: 8 (z_hi: 2, z_lo: 4; z = z_hi * 4 + z_lo), core: 2. Of those that a mesh axis runs over, the one named last changes fastest.
Arguments:
- tokens: bfloat16 [65536, 2048], P(('seq', 'sub')), may hold values from -6 to 6
- cotangent: bfloat16 [65536, 2048], P(('seq', 'sub')), may hold values from -6 to 6
- query_gain: float32 [3, 2048], replicated, may hold values from -6 to 6
- key_gain: float32 [3, 2048], replicated, may hold values from -6 to 6
Outputs:
- output: bfloat16 [65536, 2048], P(('seq', 'sub'))
- input_grad: bfloat16 [65536, 2048], P(('seq', 'sub'))
All inputs are finite; a program needn't handle non-finite values.
Results may differ from a plain program's by a relative error of at most 0.04.
Values may be sent and summed in bfloat16 or wider, within the bound.
A program may use at most 64 MiB of HBM per device.

v0:
```python
import jax
import jax.numpy as jnp
from jax import lax
from jax.sharding import PartitionSpec as P

HEADS = 16


EPSILON = 1e-06
NEGATIVE_FILL = -1e30


def passed_along(x, axis, by):
    length = lax.axis_size(axis)
    pairs = [(i, i + by) for i in range(length) if 0 <= i + by < length]
    return lax.ppermute(x, axis, pairs)


def normalize(rows_per_level):
    widened = rows_per_level.astype(jnp.float32)
    inv_rms = lax.rsqrt(jnp.mean(widened * widened, axis=-1, keepdims=True) + EPSILON)
    return ((widened * inv_rms).astype(jnp.bfloat16), inv_rms)


def norm_backward(rows_per_level, inv_rms, grad_normed):
    unit_rows = rows_per_level.astype(jnp.float32) * inv_rms
    return inv_rms * (
        grad_normed - unit_rows * jnp.mean(grad_normed * unit_rows, axis=-1, keepdims=True)
    )


def window_mask(query_pos, key_pos, window):
    ahead = query_pos[:, None] - key_pos[None, :]
    return (ahead >= 0) & (ahead < window) & (key_pos[None, :] >= 0)


def positions(first_pos, count_rows):
    return first_pos + jnp.arange(count_rows, dtype=jnp.int32)


def split_heads(matrix, head_count):
    return matrix.reshape(matrix.shape[0], head_count, matrix.shape[1] // head_count)


def head_probs(query_heads, key_heads, allowed):
    head_size = query_heads.shape[2]
    scores = jnp.einsum(
        "qhd,khd->hqk", query_heads, key_heads, preferred_element_type=jnp.float32
    ) * head_size ** (-0.5)
    scores = jnp.where(allowed[None], scores, NEGATIVE_FILL)
    row_max = jnp.max(scores, axis=-1, keepdims=True)
    weights = jnp.exp(scores - row_max)
    return weights / jnp.sum(weights, axis=-1, keepdims=True)


def gained(normed, gain):
    return (normed.astype(jnp.float32) * gain).astype(jnp.bfloat16)


def attend_rows(normed, candidates, query_gain, key_gain, allowed, head_count):
    query_rows = gained(normed, query_gain)
    key_rows = gained(candidates, key_gain)
    half_width = normed.shape[1] // 2
    half_heads = head_count // 2
    results = []
    for column_half in range(2):
        column_start = column_half * half_width
        column_end = column_start + half_width
        query_heads = split_heads(query_rows[:, column_start:column_end], half_heads)
        key_heads = split_heads(key_rows[:, column_start:column_end], half_heads)
        value_heads = split_heads(candidates[:, column_start:column_end], half_heads)
        weights = head_probs(query_heads, key_heads, allowed).astype(jnp.bfloat16)
        attended = jnp.einsum(
            "hqk,khd->qhd", weights, value_heads, preferred_element_type=jnp.float32
        )
        results.append(attended.reshape(normed.shape[0], half_width))
    return jnp.concatenate(results, axis=1)


def attend_back(normed, candidates, query_gain, key_gain, allowed, head_count, grad_out):
    query_rows = gained(normed, query_gain)
    key_rows = gained(candidates, key_gain)
    grad_rows = grad_out.astype(jnp.bfloat16)
    half_width = normed.shape[1] // 2
    half_heads = head_count // 2
    head_size = half_width // half_heads
    query_parts = []
    key_parts = []
    for column_half in range(2):
        column_start = column_half * half_width
        column_end = column_start + half_width
        query_heads = split_heads(query_rows[:, column_start:column_end], half_heads)
        key_heads = split_heads(key_rows[:, column_start:column_end], half_heads)
        value_heads = split_heads(candidates[:, column_start:column_end], half_heads)
        grad_heads = split_heads(grad_rows[:, column_start:column_end], half_heads)
        weights = head_probs(query_heads, key_heads, allowed)
        weights_low = weights.astype(jnp.bfloat16)
        d_probs = jnp.einsum(
            "qhd,khd->hqk", grad_heads, value_heads, preferred_element_type=jnp.float32
        )
        center = jnp.sum(weights * d_probs, axis=-1, keepdims=True)
        d_scores = (weights * (d_probs - center) * head_size ** (-0.5)).astype(jnp.bfloat16)
        d_query = jnp.einsum(
            "hqk,khd->qhd", d_scores, key_heads, preferred_element_type=jnp.float32
        )
        d_keys = jnp.einsum(
            "hqk,qhd->khd", d_scores, query_heads, preferred_element_type=jnp.float32
        )
        d_values = jnp.einsum(
            "hqk,qhd->khd", weights_low, grad_heads, preferred_element_type=jnp.float32
        )
        query_parts.append(
            d_query.reshape(normed.shape[0], half_width) * query_gain[column_start:column_end]
        )
        key_parts.append(
            d_keys.reshape(candidates.shape[0], half_width) * key_gain[column_start:column_end]
            + d_values.reshape(candidates.shape[0], half_width)
        )
    return (jnp.concatenate(query_parts, axis=1), jnp.concatenate(key_parts, axis=1))


def stride_list(window_extent):
    return [1] + [2**power for power in range(window_extent.bit_length() - 1)]


def fetch_previous_rows(rows_per_level, window_extent, carried_block):
    gathered_parts = rows_per_level
    for turn, pooling_factor in enumerate(stride_list(window_extent)):
        received_rows = carried_block(gathered_parts, pooling_factor)
        gathered_parts = (
            received_rows if turn == 0 else jnp.concatenate([received_rows, gathered_parts], axis=0)
        )
    return gathered_parts


def send_previous_back(summand_list, window_extent, rows_per_piece, carried_block):
    strides = stride_list(window_extent)[::-1]
    for turn, pooling_factor in enumerate(strides):
        if turn == len(strides) - 1:
            summand_list = carried_block(summand_list, pooling_factor)
        else:
            leading_rows = pooling_factor * rows_per_piece
            summand_list = summand_list[leading_rows:] + carried_block(
                summand_list[:leading_rows], pooling_factor
            )
    return summand_list


def send_full(rows_per_level, pooling_factor):
    return passed_along(rows_per_level, ("seq", "sub"), pooling_factor)


def back_full(summand_list, pooling_factor):
    return passed_along(summand_list.astype(jnp.bfloat16), ("seq", "sub"), -pooling_factor).astype(
        summand_list.dtype
    )


def send_groups(rows_per_level, pooling_factor):
    return passed_along(rows_per_level, "seq", pooling_factor)


def back_groups(summand_list, pooling_factor):
    return passed_along(summand_list.astype(jnp.bfloat16), "seq", -pooling_factor).astype(
        summand_list.dtype
    )


def pool_rows(rows_per_level):
    model_width = rows_per_level.shape[1]
    pooled = jnp.mean(rows_per_level.astype(jnp.float32).reshape(-1, 4, model_width), axis=1)
    return lax.optimization_barrier(pooled.astype(jnp.bfloat16))


def upsample(coarse, fine_count):
    edge_rows = passed_along(coarse[-1:], ("seq", "sub"), 1)
    extended = jnp.concatenate([edge_rows, coarse], axis=0)
    return jnp.repeat(extended, 4, axis=0)[1 : 1 + fine_count]


def upsample_back(grad_fine):
    model_width = grad_fine.shape[1]
    padded = jnp.concatenate(
        [
            jnp.zeros((1, model_width), jnp.float32),
            grad_fine,
            jnp.zeros((3, model_width), jnp.float32),
        ],
        axis=0,
    )
    summed = jnp.sum(padded.reshape(-1, 4, model_width), axis=1)
    edge_rows = passed_along(summed[:1], ("seq", "sub"), -1)
    own_rows = summed[1:]
    return jnp.concatenate([own_rows[:-1], own_rows[-1:] + edge_rows], axis=0)


def per_device(tokens, cotangent, query_gain, key_gain):
    full_rows = tokens.shape[0]
    head_count = HEADS
    members = lax.axis_size("sub")
    group_index = lax.axis_index("seq")
    member = lax.axis_index("sub")
    device = group_index * members + member

    def short_forward(rows_per_level, level):
        local_rows = rows_per_level.shape[0]
        normed, inv_rms = normalize(rows_per_level)
        offset = 0
        group_all = lax.all_gather(normed, "sub", axis=0, tiled=True)
        extent = group_all.shape[0]
        group_reach = full_rows // extent
        earlier = fetch_previous_rows(group_all, group_reach, send_groups)
        candidates = jnp.concatenate([earlier, group_all], axis=0)
        key_pos = positions((group_index - group_reach) * extent, candidates.shape[0])
        query_pos = positions(device * local_rows, local_rows)
        allowed = window_mask(query_pos, key_pos, full_rows)
        attended = attend_rows(
            normed, candidates, query_gain[level], key_gain[level], allowed, head_count
        )
        upper_rows = lax.optimization_barrier(
            (rows_per_level.astype(jnp.float32) + attended).astype(jnp.bfloat16)
        )
        return (upper_rows, (inv_rms, normed, candidates, allowed, offset))

    def short_backward(rows_per_level, saved_state, grad_upper, level):
        inv_rms, queries, candidates, allowed, offset = saved_state
        local_rows = rows_per_level.shape[0]
        query_term, key_term = attend_back(
            queries, candidates, query_gain[level], key_gain[level], allowed, head_count, grad_upper
        )
        extent = local_rows * members
        group_reach = full_rows // extent
        returned = send_previous_back(
            key_term[: group_reach * extent], group_reach, extent, back_groups
        )
        gathered = key_term[group_reach * extent :] + returned
        own_terms = query_term + lax.psum_scatter(
            gathered.astype(jnp.bfloat16), "sub", scatter_dimension=0, tiled=True
        ).astype(jnp.float32)
        return grad_upper + norm_backward(rows_per_level, inv_rms, own_terms)

    reach_zero = full_rows // full_rows
    normed_zero, scale_zero = normalize(tokens)
    candidates_zero = jnp.concatenate(
        [fetch_previous_rows(normed_zero, reach_zero, send_full), normed_zero], axis=0
    )
    allowed_zero = window_mask(
        positions(device * full_rows, full_rows),
        positions((device - reach_zero) * full_rows, candidates_zero.shape[0]),
        full_rows,
    )
    attended_zero = attend_rows(
        normed_zero, candidates_zero, query_gain[0], key_gain[0], allowed_zero, head_count
    )
    upper_zero = lax.optimization_barrier(
        (tokens.astype(jnp.float32) + attended_zero).astype(jnp.bfloat16)
    )
    first_input = pool_rows(upper_zero)
    upper_one, saved_one = short_forward(first_input, 1)
    second_input = pool_rows(upper_one)
    upper_two, saved_two = short_forward(second_input, 2)
    middle = (
        upper_one.astype(jnp.float32) + upsample(upper_two, upper_one.shape[0]).astype(jnp.float32)
    ).astype(jnp.bfloat16)
    middle = lax.optimization_barrier(middle)
    output = (
        upper_zero.astype(jnp.float32) + upsample(middle, full_rows).astype(jnp.float32)
    ).astype(jnp.bfloat16)
    grad_top = cotangent.astype(jnp.float32)
    grad_middle = upsample_back(grad_top)
    grad_two = upsample_back(grad_middle)
    back_two = short_backward(second_input, saved_two, grad_two, 2)
    grad_one = grad_middle + jnp.repeat(back_two, 4, axis=0) * 0.25
    back_one = short_backward(first_input, saved_one, grad_one, 1)
    grad_zero = grad_top + jnp.repeat(back_one, 4, axis=0) * 0.25
    query_term, key_term = attend_back(
        normed_zero,
        candidates_zero,
        query_gain[0],
        key_gain[0],
        allowed_zero,
        head_count,
        grad_zero,
    )
    returned = send_previous_back(
        key_term[: reach_zero * full_rows], reach_zero, full_rows, back_full
    )
    own_terms = query_term + key_term[reach_zero * full_rows :] + returned
    input_grad = (grad_zero + norm_backward(tokens, scale_zero, own_terms)).astype(jnp.bfloat16)
    return (output, input_grad)


def solution(mesh):
    placed = (P(("seq", "sub"), None), P(("seq", "sub"), None), P(), P())
    return jax.shard_map(
        per_device,
        mesh=mesh,
        in_specs=placed,
        out_specs=(P(("seq", "sub"), None), P(("seq", "sub"), None)),
        check_vma=False,
    )
```

profile of v0, /device:TPU:1, one launch (start us, length us, event | category | flops | bytes accessed | tf_op | source)
XLA Modules:
  0.0 362.6 jit_solution(15498596107546719899)
XLA Ops:
  11.6 4.8 %collective-permute-start = (bf16[128,2048]{0,1:T(8,128)(2,1)}, bf16[128,2048]{0,1:T(8,128)(2,1)}, u32[]{:S(2)}, u32[]{:S(2)}) collective-permute-start(bf16[128,2048]{0,1:T(8,128)(2,1)} %get-tuple-element.15), channel_id=1, source_target_pairs={{0,1},{1,2},{2,3},{3,4},{4,5},{5,6},{6,7},{7,8},{8,9},{9,10},{10,1... | collective-permute-start | bytes 1572872 | tf_op jit(solution)/shard_map/ppermute | solution.py:16
  22.6 6.1 %collective-permute-start.7 = (f32[1,2048]{1,0:T(1,128)}, f32[1,2048]{1,0:T(1,128)}, u32[]{:S(2)}, u32[]{:S(2)}) collective-permute-start(f32[1,2048]{1,0:T(1,128)} %slice.333), channel_id=1, source_target_pairs={{1,0},{2,1},{3,2},{4,3},{5,4},{6,5},{7,6},{8,7},{9,8},{10,9},{11,1... | collective-permute-start | bytes 24584 | tf_op jit(solution)/shard_map/ppermute | solution.py:16
  30.4 2.4 collective-permute-done
  39.8 2.8 fusion.253
  49.2 14.0 %all_gather.6 = bf16[128,2048]{1,0:T(8,128)(2,1)S(1)} all-gather(bf16[32,2048]{1,0:T(8,128)(2,1)S(1)} %get-tuple-element.13), channel_id=1, replica_groups=mesh['seq'=128,'sub'=4] {'sub'}, dimensions={0}, use_global_device_ids=true | all-gather | bytes 655360 | tf_op jit(solution)/shard_map/all_gather | solution.py:209
  63.5 5.0 %collective-permute-start.1 = (bf16[128,2048]{0,1:T(8,128)(2,1)S(1)}, bf16[128,2048]{0,1:T(8,128)(2,1)S(1)}, u32[]{:S(2)}, u32[]{:S(2)}) collective-permute-start(bf16[128,2048]{0,1:T(8,128)(2,1)S(1)} %copy.168), channel_id=1, source_target_pairs={{0,4},{4,8},{8,12},{12,16},{16,20},{20,24},{24,28},{28,32},{32,36}... | collective-permute-start | bytes 1572872 | tf_op jit(solution)/shard_map/ppermute | solution.py:16
  71.0 3.6 collective-permute-done.1
  79.2 10.5 %all_gather.7 = bf16[32,2048]{1,0:T(8,128)(2,1)S(1)} all-gather(bf16[8,2048]{1,0:T(8,128)(2,1)S(1)} %get-tuple-element.11), channel_id=1, replica_groups=mesh['seq'=128,'sub'=4] {'sub'}, dimensions={0}, use_global_device_ids=true | all-gather | bytes 163840 | tf_op jit(solution)/shard_map/all_gather | solution.py:209
  89.6 7.3 %collective-permute-start.2 = (bf16[32,2048]{1,0:T(8,128)(2,1)S(1)}, bf16[32,2048]{1,0:T(8,128)(2,1)S(1)}, u32[]{:S(2)}, u32[]{:S(2)}) collective-permute-start(bf16[32,2048]{1,0:T(8,128)(2,1)S(1)} %all_gather.7), channel_id=1, source_target_pairs={{0,4},{4,8},{8,12},{12,16},{16,20},{20,24},{24,28},{28,32},{32,36}... | collective-permute-start | bytes 393224 | tf_op jit(solution)/shard_map/ppermute | solution.py:16
  98.9 4.3 %collective-permute-start.3 = (bf16[32,2048]{1,0:T(8,128)(2,1)S(1)}, bf16[32,2048]{1,0:T(8,128)(2,1)S(1)}, u32[]{:S(2)}, u32[]{:S(2)}) collective-permute-start(bf16[32,2048]{1,0:T(8,128)(2,1)S(1)} %collective-permute-done.2), channel_id=1, source_target_pairs={{0,4},{4,8},{8,12},{12,16},{16,20},{20,24},{24,28},{28,32},{32,36}... | collective-permute-start | bytes 393224 | tf_op jit(solution)/shard_map/ppermute | solution.py:16
  105.6 3.6 collective-permute-start.4
  109.2 4.0 %collective-permute-done.4 = bf16[64,2048]{1,0:T(8,128)(2,1)S(1)} collective-permute-done((bf16[64,2048]{1,0:T(8,128)(2,1)S(1)}, bf16[64,2048]{1,0:T(8,128)(2,1)S(1)}, u32[]{:S(2)}, u32[]{:S(2)}) %collective-permute-start.4) | collective-permute-done | bytes 262176 | tf_op jit(solution)/shard_map/ppermute | solution.py:16
  126.3 11.9 %collective-permute-done.9 = bf16[64,2048]{1,0:T(8,128)(2,1)S(1)} collective-permute-done((bf16[64,2048]{1,0:T(8,128)(2,1)S(1)}, bf16[64,2048]{1,0:T(8,128)(2,1)S(1)}, u32[]{:S(2)}, u32[]{:S(2)}) %collective-permute-start.9) | collective-permute-done | bytes 262176 | tf_op jit(solution)/shard_map/ppermute | solution.py:16
  142.6 3.4 collective-permute-done.10
  150.9 2.5 collective-permute-done.11
  156.6 64.6 %reduce-scatter.5.cloned.1.call-done = bf16[8,2048]{1,0:T(8,128)(2,1)} async-done(((bf16[32,2048]{1,0:T(8,128)(2,1)}), bf16[8,2048]{1,0:T(8,128)(2,1)}) %reduce-scatter.5.cloned.1.call-update) | async-done | bytes 32784 | tf_op jit(solution)/shard_map/reduce_scatter | solution.py:237
  225.2 2.8 convolution_bitcast_fusion.5
  228.0 3.4 fusion.74
  233.4 2.8 fusion.172
  239.5 3.4 fusion.75
  245.8 4.8 %collective-permute-start.12 = (bf16[128,2048]{0,1:T(8,128)(2,1)}, bf16[128,2048]{0,1:T(8,128)(2,1)}, u32[]{:S(2)}, u32[]{:S(2)}) collective-permute-start(bf16[128,2048]{0,1:T(8,128)(2,1)} %fusion.73), channel_id=1, source_target_pairs={{4,0},{8,4},{12,8},{16,12},{20,16},{24,20},{28,24},{32,28},{36,32}... | collective-permute-start | bytes 1572872 | tf_op jit(solution)/shard_map/ppermute | solution.py:16
  251.2 3.1 convolution_bitcast_fusion.4
  263.9 3.0 collective-permute-start.6
  267.9 2.8 collective-permute-done.6
  274.6 20.9 %reduce-scatter.7.cloned.1.call-done = bf16[32,2048]{1,0:T(8,128)(2,1)} async-done(((bf16[128,2048]{1,0:T(8,128)(2,1)}), bf16[32,2048]{1,0:T(8,128)(2,1)}) %reduce-scatter.7.cloned.1.call-update) | async-done | bytes 131088 | tf_op jit(solution)/shard_map/reduce_scatter | solution.py:237
  300.1 8.0 %fusion.77 = f32[8,128,128]{2,1,0:T(8,128)} fusion(bf16[256,8,128]{0,2,1:T(8,128)(2,1)} %bitcast.294, f32[8,128,256]{2,1,0:T(8,128)S(1)} %fusion.262, f32[8,128,256]{2,1,0:T(8,128)} %get-tuple-element.59, f32[8,128]{1,0:T(8,128)S(1)} %copy-done.86), kind=kOutput, calls=%fused_computation.132 | convolution fusion | flops 68945152 | bytes 3149824 | tf_op jit(solution)/shard_map/hqk,khd->qhd/dot_general | solution.py:103
  308.1 8.1 %fusion.76 = f32[8,128,256]{2,1,0:T(8,128)} fusion(bf16[128,8,128]{0,2,1:T(8,128)(2,1)} %bitcast.304, f32[8,128,256]{2,1,0:T(8,128)S(1)} %fusion.262, f32[8,128,256]{2,1,0:T(8,128)} %get-tuple-element.59, f32[8,128]{1,0:T(8,128)S(1)} %copy-done.86), kind=kOutput, calls=%fused_computation.131 | convolution fusion | flops 68945152 | bytes 3411968 | tf_op jit(solution)/shard_map/hqk,qhd->khd/dot_general | solution.py:106
  316.2 3.1 fusion.144
  320.8 2.8 fusion.140
  323.6 8.6 %fusion.82 = f32[8,128,256]{2,1,0:T(8,128)} fusion(bf16[128,8,128]{0,2,1:T(8,128)(2,1)S(1)} %bitcast.302, f32[8,128,256]{2,1,0:T(8,128)} %fusion.263, f32[8,128,256]{2,1,0:T(8,128)} %get-tuple-element.57, f32[8,128]{1,0:T(8,128)S(1)} %copy-done.84), kind=kOutput, calls=%fused_computation.136 | convolution fusion | flops 68945152 | bytes 3411968 | tf_op jit(solution)/shard_map/hqk,qhd->khd/dot_general | solution.py:106
  336.5 4.2 %collective-permute-start.13 = (bf16[128,2048]{0,1:T(8,128)(2,1)}, bf16[128,2048]{0,1:T(8,128)(2,1)}, u32[]{:S(2)}, u32[]{:S(2)}) collective-permute-start(bf16[128,2048]{0,1:T(8,128)(2,1)} %fusion.72), channel_id=1, source_target_pairs={{1,0},{2,1},{3,2},{4,3},{5,4},{6,5},{7,6},{8,7},{9,8},{10,9},{11,1... | collective-permute-start | bytes 1572872 | tf_op jit(solution)/shard_map/ppermute | solution.py:16
  341.7 8.6 %fusion.83 = f32[8,128,128]{2,1,0:T(8,128)} fusion(bf16[256,8,128]{0,2,1:T(8,128)(2,1)} %bitcast.291, f32[8,128,256]{2,1,0:T(8,128)} %fusion.263, f32[8,128,256]{2,1,0:T(8,128)} %get-tuple-element.57, f32[8,128]{1,0:T(8,128)S(1)} %copy-done.84), kind=kOutput, calls=%fused_computation.137 | convolution fusion | flops 68945152 | bytes 3149824 | tf_op jit(solution)/shard_map/hqk,khd->qhd/dot_general | solution.py:103
  (341 shorter events, 105.7 us)
Async XLA Ops:
  7.2 214.1 %reduce-scatter.5.cloned.1.call-start = ((), (), s32[]{:S(2)}) async-start(), calls=%async_computation.2 | async-start | bytes 163840 | tf_op jit(solution)/shard_map/reduce_scatter | solution.py:237
  11.6 21.2 %collective-permute-start = (bf16[128,2048]{0,1:T(8,128)(2,1)}, bf16[128,2048]{0,1:T(8,128)(2,1)}, u32[]{:S(2)}, u32[]{:S(2)}) collective-permute-start(bf16[128,2048]{0,1:T(8,128)(2,1)} %get-tuple-element.15), channel_id=1, source_target_pairs={{0,1},{1,2},{2,3},{3,4},{4,5},{5,6},{6,7},{7,8},{8,9},{9,10},{10,1... | collective-permute-start | bytes 1572872 | tf_op jit(solution)/shard_map/ppermute | solution.py:16
  21.9 48.4 %copy-start.26 = (f32[33,2048]{1,0:T(8,128)}, f32[33,2048]{1,0:T(8,128)S(1)}, u32[]{:S(2)}) copy-start(f32[33,2048]{1,0:T(8,128)S(1)} %reduce_sum.233) | copy-start | bytes 811012
  22.6 74.4 %collective-permute-start.7 = (f32[1,2048]{1,0:T(1,128)}, f32[1,2048]{1,0:T(1,128)}, u32[]{:S(2)}, u32[]{:S(2)}) collective-permute-start(f32[1,2048]{1,0:T(1,128)} %slice.333), channel_id=1, source_target_pairs={{1,0},{2,1},{3,2},{4,3},{5,4},{6,5},{7,6},{8,7},{9,8},{10,9},{11,1... | collective-permute-start | bytes 24584 | tf_op jit(solution)/shard_map/ppermute | solution.py:16
  29.7 12.8 %copy-start.59 = (pred[128,256]{1,0:T(8,128)(4,1)}, pred[128,256]{1,0:T(8,128)(4,1)S(1)}, u32[]{:S(2)}) copy-start(pred[128,256]{1,0:T(8,128)(4,1)S(1)} %fusion.153) | copy-start | bytes 98308
  48.3 20.9 %copy-start.82 = (f32[3]{0:T(128)S(1)}, f32[3]{0:T(128)}, u32[]{:S(2)}) copy-start(f32[3]{0:T(128)} %copy-done.81) | copy-start | bytes 40
  49.1 25.9 %copy-start.76 = (f32[32]{0:T(128)}, f32[32]{0:T(128)S(1)}, u32[]{:S(2)}) copy-start(f32[32]{0:T(128)S(1)} %add_rsqrt_fusion.1) | copy-start | bytes 388
  63.5 11.1 %collective-permute-start.1 = (bf16[128,2048]{0,1:T(8,128)(2,1)S(1)}, bf16[128,2048]{0,1:T(8,128)(2,1)S(1)}, u32[]{:S(2)}, u32[]{:S(2)}) collective-permute-start(bf16[128,2048]{0,1:T(8,128)(2,1)S(1)} %copy.168), channel_id=1, source_target_pairs={{0,4},{4,8},{8,12},{12,16},{16,20},{20,24},{24,28},{28,32},{32,36}... | collective-permute-start | bytes 1572872 | tf_op jit(solution)/shard_map/ppermute | solution.py:16
  78.0 25.2 %copy-start.79 = (f32[36]{0:T(128)S(1)}, f32[36]{0:T(128)}, u32[]{:S(2)}) copy-start(f32[36]{0:T(128)} %pad.17.clone) | copy-start | bytes 436
  78.0 25.2 %copy-start.80 = (f32[36]{0:T(128)S(1)}, f32[36]{0:T(128)}, u32[]{:S(2)}) copy-start(f32[36]{0:T(128)} %pad.14.clone) | copy-start | bytes 436
  78.6 20.2 %copy-start.24 = (bf16[32,2048]{1,0:T(8,128)(2,1)}, bf16[32,2048]{1,0:T(8,128)(2,1)S(1)}, u32[]{:S(2)}) copy-start(bf16[32,2048]{1,0:T(8,128)(2,1)S(1)} %fusion.134) | copy-start | bytes 393220
  79.1 24.6 %copy-start.75 = (f32[8]{0:T(128)}, f32[8]{0:T(128)S(1)}, u32[]{:S(2)}) copy-start(f32[8]{0:T(128)S(1)} %add_rsqrt_fusion) | copy-start | bytes 100
  79.2 38.1 %copy-start.54 = (bf16[8,2048]{1,0:T(8,128)(2,1)}, bf16[8,2048]{1,0:T(8,128)(2,1)S(1)}, u32[]{:S(2)}) copy-start(bf16[8,2048]{1,0:T(8,128)(2,1)S(1)} %get-tuple-element.10) | copy-start | bytes 98308
  89.6 9.2 %collective-permute-start.2 = (bf16[32,2048]{1,0:T(8,128)(2,1)S(1)}, bf16[32,2048]{1,0:T(8,128)(2,1)S(1)}, u32[]{:S(2)}, u32[]{:S(2)}) collective-permute-start(bf16[32,2048]{1,0:T(8,128)(2,1)S(1)} %all_gather.7), channel_id=1, source_target_pairs={{0,4},{4,8},{8,12},{12,16},{16,20},{20,24},{24,28},{28,32},{32,36}... | collective-permute-start | bytes 393224 | tf_op jit(solution)/shard_map/ppermute | solution.py:16
  98.9 6.7 %collective-permute-start.3 = (bf16[32,2048]{1,0:T(8,128)(2,1)S(1)}, bf16[32,2048]{1,0:T(8,128)(2,1)S(1)}, u32[]{:S(2)}, u32[]{:S(2)}) collective-permute-start(bf16[32,2048]{1,0:T(8,128)(2,1)S(1)} %collective-permute-done.2), channel_id=1, source_target_pairs={{0,4},{4,8},{8,12},{12,16},{16,20},{20,24},{24,28},{28,32},{32,36}... | collective-permute-start | bytes 393224 | tf_op jit(solution)/shard_map/ppermute | solution.py:16
  103.7 5.5 %collective-permute-start.8 = (f32[1,2048]{1,0:T(1,128)S(1)}, f32[1,2048]{1,0:T(1,128)S(1)}, u32[]{:S(2)}, u32[]{:S(2)}) collective-permute-start(f32[1,2048]{1,0:T(1,128)S(1)} %slice.336), channel_id=1, source_target_pairs={{1,0},{2,1},{3,2},{4,3},{5,4},{6,5},{7,6},{8,7},{9,8},{10,9},{11,1... | collective-permute-start | bytes 24584 | tf_op jit(solution)/shard_map/ppermute | solution.py:16
  105.6 7.6 %collective-permute-start.4 = (bf16[64,2048]{1,0:T(8,128)(2,1)S(1)}, bf16[64,2048]{1,0:T(8,128)(2,1)S(1)}, u32[]{:S(2)}, u32[]{:S(2)}) collective-permute-start(bf16[64,2048]{1,0:T(8,128)(2,1)S(1)} %pad_maximum_fusion.5), channel_id=1, source_target_pairs={{0,8},{4,12},{8,16},{12,20},{16,24},{20,28},{24,32},{28,36},{32,40... | collective-permute-start | bytes 786440 | tf_op jit(solution)/shard_map/ppermute | solution.py:16
  124.3 17.0 %copy-start.44 = (f32[8,8,160]{2,1,0:T(8,128)S(1)}, f32[8,8,160]{2,1,0:T(8,128)}, u32[]{:S(2)}) copy-start(f32[8,8,160]{2,1,0:T(8,128)} %get-tuple-element.65) | copy-start | bytes 122884
  124.3 17.0 %copy-start.45 = (f32[8,8,160]{2,1,0:T(8,128)S(1)}, f32[8,8,160]{2,1,0:T(8,128)}, u32[]{:S(2)}) copy-start(f32[8,8,160]{2,1,0:T(8,128)} %fusion.117) | copy-start | bytes 122884
  124.4 13.9 %collective-permute-start.9 = (bf16[64,2048]{1,0:T(8,128)(2,1)S(1)}, bf16[64,2048]{1,0:T(8,128)(2,1)S(1)}, u32[]{:S(2)}, u32[]{:S(2)}) collective-permute-start(bf16[64,2048]{1,0:T(8,128)(2,1)S(1)} %fusion.94), channel_id=1, source_target_pairs={{8,0},{12,4},{16,8},{20,12},{24,16},{28,20},{32,24},{36,28},{40,32... | collective-permute-start | bytes 786440 | tf_op jit(solution)/shard_map/ppermute | solution.py:16
  138.9 7.1 %collective-permute-start.10 = (bf16[32,2048]{1,0:T(8,128)(2,1)}, bf16[32,2048]{1,0:T(8,128)(2,1)}, u32[]{:S(2)}, u32[]{:S(2)}) collective-permute-start(bf16[32,2048]{1,0:T(8,128)(2,1)} %slice.442), channel_id=1, source_target_pairs={{4,0},{8,4},{12,8},{16,12},{20,16},{24,20},{28,24},{32,28},{36,32}... | collective-permute-start | bytes 393224 | tf_op jit(solution)/shard_map/ppermute | solution.py:16
  147.0 6.4 %collective-permute-start.11 = (bf16[32,2048]{1,0:T(8,128)(2,1)S(1)}, bf16[32,2048]{1,0:T(8,128)(2,1)S(1)}, u32[]{:S(2)}, u32[]{:S(2)}) collective-permute-start(bf16[32,2048]{1,0:T(8,128)(2,1)S(1)} %fusion.138), channel_id=1, source_target_pairs={{4,0},{8,4},{12,8},{16,12},{20,16},{24,20},{28,24},{32,28},{36,32}... | collective-permute-start | bytes 393224 | tf_op jit(solution)/shard_map/ppermute | solution.py:16
  154.1 70.5 %copy-start.18 = (bf16[256,1024]{0,1:T(8,128)(2,1)S(1)}, bf16[256,1024]{0,1:T(8,128)(2,1)}, u32[]{:S(2)}) copy-start(bf16[256,1024]{0,1:T(8,128)(2,1)} %copy-done.17) | copy-start | bytes 1572868
  154.1 141.4 %reduce-scatter.7.cloned.1.call-start = ((), (), s32[]{:S(2)}) async-start(), calls=%async_computation.3 | async-start | bytes 655360 | tf_op jit(solution)/shard_map/reduce_scatter | solution.py:237
  155.3 69.9 %copy-start.14 = (bf16[256,1024]{0,1:T(8,128)(2,1)S(1)}, bf16[256,1024]{0,1:T(8,128)(2,1)}, u32[]{:S(2)}) copy-start(bf16[256,1024]{0,1:T(8,128)(2,1)} %copy-done.13) | copy-start | bytes 1572868
  237.5 16.8 %collective-permute-start.5 = (bf16[1,2048]{1,0:T(2,128)(2,1)}, bf16[1,2048]{1,0:T(2,128)(2,1)}, u32[]{:S(2)}, u32[]{:S(2)}) collective-permute-start(bf16[1,2048]{1,0:T(2,128)(2,1)} %slice.327), channel_id=1, source_target_pairs={{0,1},{1,2},{2,3},{3,4},{4,5},{5,6},{6,7},{7,8},{8,9},{9,10},{10,1... | collective-permute-start | bytes 12296 | tf_op jit(solution)/shard_map/ppermute | solution.py:16
  245.8 13.1 %collective-permute-start.12 = (bf16[128,2048]{0,1:T(8,128)(2,1)}, bf16[128,2048]{0,1:T(8,128)(2,1)}, u32[]{:S(2)}, u32[]{:S(2)}) collective-permute-start(bf16[128,2048]{0,1:T(8,128)(2,1)} %fusion.73), channel_id=1, source_target_pairs={{4,0},{8,4},{12,8},{16,12},{20,16},{24,20},{28,24},{32,28},{36,32}... | collective-permute-start | bytes 1572872 | tf_op jit(solution)/shard_map/ppermute | solution.py:16
  263.9 6.8 %collective-permute-start.6 = (bf16[1,2048]{1,0:T(2,128)(2,1)S(1)}, bf16[1,2048]{1,0:T(2,128)(2,1)S(1)}, u32[]{:S(2)}, u32[]{:S(2)}) collective-permute-start(bf16[1,2048]{1,0:T(2,128)(2,1)S(1)} %slice.329), channel_id=1, source_target_pairs={{0,1},{1,2},{2,3},{3,4},{4,5},{5,6},{6,7},{7,8},{8,9},{9,10},{10,1... | collective-permute-start | bytes 12296 | tf_op jit(solution)/shard_map/ppermute | solution.py:16
  272.0 23.5 %copy-start.25 = (f32[32,1024]{1,0:T(8,128)S(1)}, f32[32,1024]{1,0:T(8,128)}, u32[]{:S(2)}) copy-start(f32[32,1024]{1,0:T(8,128)} %bitcast_multiply_fusion.9) | copy-start | bytes 393220
  272.1 23.5 %copy-start.77 = (f32[32]{0:T(128)S(1)}, f32[32]{0:T(128)}, u32[]{:S(2)}) copy-start(f32[32]{0:T(128)} %copy-done.76) | copy-start | bytes 388
  272.1 24.6 %copy-start.6 = (f32[32,2048]{1,0:T(8,128)S(1)}, f32[32,2048]{1,0:T(8,128)}, u32[]{:S(2)}) copy-start(f32[32,2048]{1,0:T(8,128)} %copy-done.5) | copy-start | bytes 786436
  336.5 16.3 %collective-permute-start.13 = (bf16[128,2048]{0,1:T(8,128)(2,1)}, bf16[128,2048]{0,1:T(8,128)(2,1)}, u32[]{:S(2)}, u32[]{:S(2)}) collective-permute-start(bf16[128,2048]{0,1:T(8,128)(2,1)} %fusion.72), channel_id=1, source_target_pairs={{1,0},{2,1},{3,2},{4,3},{5,4},{6,5},{7,6},{8,7},{9,8},{10,9},{11,1... | collective-permute-start | bytes 1572872 | tf_op jit(solution)/shard_map/ppermute | solution.py:16
  (71 other events, 312.1 us)
Sparse Core Ops, SparseCore 0:
  154.2 67.0 reduce-scatter.4
  263.0 32.4 reduce-scatter.6
where the time goes:
time: 365 us; the launch traced here: 363 us
  waiting for transfers between devices  120 us (33%)
  matrix products  81.9 us (22%)
  starting transfers between devices  52.7 us (14%)
  other arithmetic  36.6 us (10%)
  local copies, waits for them, and re-layouts  31.5 us (9%)
  blocking collectives  24.5 us (7%)
  between operations  15.5 us (4%)
    reduce_scatter x2, waiting for transfers between devices, short_backward(): lax.psum_scatter(gathered.astype(jnp.bfloat16), 'sub', scatter_dimension=...  85.6 us
    ppermute x14, starting transfers between devices, passed_along(): return lax.ppermute(x, axis, pairs)  52.6 us
    ppermute x14, waiting for transfers between devices, passed_along(): return lax.ppermute(x, axis, pairs)  34.2 us
    dot_general x6, matrix products, attend_back(): jnp.einsum('hqk,qhd->khd', d_scores, query_heads, preferred_element_type=...  27.3 us
    dot_general x6, matrix products, attend_back(): jnp.einsum('hqk,khd->qhd', d_scores, key_heads, preferred_element_type=jn...  25.2 us
    all_gather x2, blocking collectives, short_forward(): group_all = lax.all_gather(normed, 'sub', axis=0, tiled=True)  24.5 us
    dot_general x6, matrix products, attend_back(): jnp.einsum('hqk,qhd->khd', weights_low, grad_heads, preferred_element_typ...  12.1 us
    unnamed x187, local copies, waits for them, and re-layouts  11.3 us
  transfers between devices with their start and end apart: 16, of which 12 were waited for; matrix products, arithmetic and copies ran while one was open for 19% of the time, Pallas kernels for 0%

commit v1 on v0

v1 whole, which is shorter than its diff:
```python
import jax
import jax.numpy as jnp
from jax import lax
from jax.experimental import pallas as pl
from jax.experimental.pallas import tpu as pltpu
from jax.sharding import PartitionSpec as P

HEADS = 16
EPSILON = 1e-06
NEGATIVE_FILL = -1e30
HEAD = 128
ROWS = 128
WIDTH = HEADS * HEAD
MEMBERS = 4
COLS = WIDTH // MEMBERS
MESH = pl.DeviceIdType.MESH
F32 = jnp.float32
BF16 = jnp.bfloat16


def multiple(value, by):
    return pl.multiple_of(value, by)


def iotas(rows, columns):
    shape = (rows, columns)
    return lax.broadcasted_iota(jnp.int32, shape, 0), lax.broadcasted_iota(jnp.int32, shape, 1)


def ones_where(mask):
    return jnp.where(mask, 1.0, 0.0).astype(BF16)


def dot(a, b):
    return lax.dot_general(a, b, (((1,), (0,)), ((), ())), preferred_element_type=F32)


def dot_t(a, b):
    return lax.dot_general(a, b, (((1,), (1,)), ((), ())), preferred_element_type=F32)


def t_dot(a, b):
    return lax.dot_general(a, b, (((0,), (0,)), ((), ())), preferred_element_type=F32)


def split_dot(ones, x):
    high = x.astype(BF16)
    low = (x - high.astype(F32)).astype(BF16)
    return dot(ones, high) + dot(ones, low)


def own_mask():
    query, key = iotas(ROWS, ROWS)
    return key <= query


def gained(normed, gain):
    return (normed.astype(F32) * gain).astype(BF16)


def head_forward(cur, prev, query_gain, key_gain, prev_bias):
    own = own_mask()
    query = gained(cur, query_gain)
    scale = HEAD ** (-0.5)
    scores = jnp.where(
        own,
        dot_t(query, gained(cur, key_gain)) * scale,
        dot_t(query, gained(prev, key_gain)) * scale + prev_bias,
    )
    weights = jnp.exp(scores - jnp.max(scores, axis=-1, keepdims=True))
    probs = weights / jnp.sum(weights, axis=-1, keepdims=True)
    zero = jnp.zeros_like(probs)
    attended = dot(jnp.where(own, probs, zero).astype(BF16), cur) + dot(
        jnp.where(own, zero, probs).astype(BF16), prev
    )
    return probs, attended


def head_backward(cur, prev, query_gain, key_gain, probs, grad):
    own = own_mask()
    query = gained(cur, query_gain)
    zero = jnp.zeros_like(probs)
    d_probs = jnp.where(own, dot_t(grad, cur), dot_t(grad, prev))
    center = jnp.sum(probs * d_probs, axis=-1, keepdims=True)
    d_scores = probs * (d_probs - center) * HEAD ** (-0.5)
    ds_cur = jnp.where(own, d_scores, zero).astype(BF16)
    ds_prev = jnp.where(own, zero, d_scores).astype(BF16)
    p_cur = jnp.where(own, probs, zero).astype(BF16)
    p_prev = jnp.where(own, zero, probs).astype(BF16)
    d_query = dot(ds_cur, gained(cur, key_gain)) + dot(ds_prev, gained(prev, key_gain))
    term_cur = d_query * query_gain + t_dot(ds_cur, query) * key_gain + t_dot(p_cur, grad)
    term_prev = t_dot(ds_prev, query) * key_gain + t_dot(p_prev, grad)
    return term_cur, term_prev


def fold(x):
    return sum(x[:, HEAD * k : HEAD * (k + 1)] for k in range(COLS // HEAD))


def up_matrix():
    row, col = iotas(ROWS, 48)
    inside = (col < 32) & (row >= 4 * col + 3) & (row <= 4 * col + 6)
    return ones_where(inside | ((col == 32) & (row <= 2)))


def repeat_matrix():
    row, col = iotas(ROWS, 32)
    return ones_where((row >= 4 * col) & (row < 4 * col + 4))


def pool_matrix():
    row, col = iotas(32, ROWS)
    return ones_where((col >= 4 * row) & (col < 4 * row + 4))


def kernel(
    groups, tokens_hbm, cot_hbm, qg, kg, out_hbm, grad_hbm,
    tok, cotx, n0, n0p, u0, p0, inv0, gc0, gp0, gr0, g0, out_v,
    h1r, n1r, n1c, n1p, h1, p1, u1, u1_in, gmr, g2r, gmh, g2h,
    sq, sq_in, n2r, n2c, n2p, gl2, gl2h, c2, gp2, r2c, r2p, dz, dz_in,
    u2x, edge, edge_in, midx, midr, b2, b2r, gl1, gc1, gp1, gr1, g1s, g1r, gl0,
    local_sem, send_sem, recv_sem,
):
    seq = lax.axis_index("seq")
    sub = lax.axis_index("sub")
    devices = groups * MEMBERS
    device = seq * MEMBERS + sub
    in_unit = lax.rem(seq, 4)
    unit_base = seq - in_unit

    def at_seq(s):
        return (lax.rem(s + groups, groups), sub)

    def at_device(d):
        d = lax.rem(d + devices, devices)
        return (lax.div(d, MEMBERS), lax.rem(d, MEMBERS))

    def peer(k):
        return lax.rem(sub + k, MEMBERS)

    used = [0]
    sent = []

    def take(count):
        used[0] += count
        return used[0] - count

    def remote(src, dst, index, target):
        return pltpu.make_async_remote_copy(
            src_ref=src, dst_ref=dst, send_sem=send_sem.at[index], recv_sem=recv_sem.at[index],
            device_id=target, device_id_type=MESH,
        )

    def post(src, dst, target):
        copy = remote(src, dst, take(1), target)
        copy.start()
        sent.append(copy)
        return copy

    def to_members(source, target_ref):
        return [post(source(peer(k)), target_ref, (seq, peer(k))) for k in range(1, MEMBERS)]

    def arrived(copies):
        for copy in copies:
            copy.wait_recv()

    def cols(member):
        return pl.ds(multiple(member * COLS, COLS), COLS)

    def rows(index, count):
        return pl.ds(multiple(index * count, count), count)

    load_tok = pltpu.make_async_copy(tokens_hbm, tok, local_sem.at[0])
    load_cot = pltpu.make_async_copy(cot_hbm, cotx.at[pl.ds(0, ROWS)], local_sem.at[1])
    load_tok.start()
    load_cot.start()
    barrier = pltpu.get_barrier_semaphore()
    partners = [at_device(device + 1), at_device(device - 1)]
    partners += [(seq, peer(k)) for k in range(1, MEMBERS)]
    partners += [at_seq(unit_base + lax.rem(in_unit + k, 4)) for k in range(1, 4)]
    partners += [at_seq(unit_base + 4 + k) for k in range(4)]
    partners += [at_seq(unit_base - 4 + k) for k in range(4)]
    for partner in partners:
        pl.semaphore_signal(barrier, inc=1, device_id=partner, device_id_type=MESH)

    load_tok.wait()

    def normalize_rows(block, _):
        here = pl.ds(multiple(block * 16, 16), 16)
        x = tok[here, :].astype(F32)
        inv = lax.rsqrt(jnp.sum(x * x, axis=-1, keepdims=True) / WIDTH + EPSILON)
        inv0[here, :] = inv
        n0[here, :] = (x * inv).astype(BF16)
        return 0

    lax.fori_loop(0, ROWS // 16, normalize_rows, 0)
    pl.semaphore_wait(barrier, len(partners))

    halo_index = take(4)

    def halo(chunk):
        here = cols(chunk)
        return remote(n0.at[:, here], n0p.at[:, here], halo_index + chunk, at_device(device + 1))

    for chunk in range(4):
        halo(chunk).start()
    load_cot.wait()
    cot_edge = post(
        cotx.at[pl.ds(0, 16)], cotx.at[pl.ds(ROWS, 16)], at_device(device - 1)
    )

    bias0 = jnp.where(device > 0, 0.0, NEGATIVE_FILL).astype(F32)

    def forward_chunk(chunk, _):
        halo(chunk).wait_recv()
        for k in range(4):
            here = pl.ds(multiple(chunk * COLS + k * HEAD, HEAD), HEAD)
            probs, attended = head_forward(
                n0[:, here], n0p[:, here], qg[0:1, here], kg[0:1, here], bias0
            )
            p0[chunk * 4 + k] = probs
            u0[:, here] = (tok[:, here].astype(F32) + attended).astype(BF16)
        h1r[:, cols(chunk)] = (dot(pool_matrix(), u0[:, cols(chunk)]) * 0.25).astype(BF16)
        return 0

    lax.fori_loop(0, 4, forward_chunk, 0)

    h1_rows = h1r[...].astype(F32)
    inv1 = lax.rsqrt(jnp.sum(h1_rows * h1_rows, axis=-1, keepdims=True) / WIDTH + EPSILON)
    n1r[...] = (h1_rows * inv1).astype(BF16)
    n1_copies = to_members(lambda t: n1r.at[:, cols(t)], n1c.at[rows(sub, 32)])
    h1_copies = to_members(lambda t: h1r.at[:, cols(t)], h1.at[rows(sub, 32)])
    n1c[rows(sub, 32), :] = n1r[:, cols(sub)]
    h1[rows(sub, 32), :] = h1r[:, cols(sub)]

    cot_edge.wait_recv()
    row, col = iotas(48, ROWS + 16)
    known = (col < ROWS) | (device < devices - 1)
    first = (row < 32) & (col >= 4 * row + 3) & (col <= 4 * row + 6)
    start = 16 * (row - 32) + 15
    second = (row >= 32) & (row < 40) & (col >= start) & (col < start + 16)
    gather = ones_where(known & (first | second))
    for chunk in range(4):
        here = pl.ds(chunk * COLS, COLS)
        summed = dot(gather, cotx[:, here])
        gmr[:, here] = summed[0:32]
        g2r[:, here] = summed[32:40]
    gm_low = u1_in
    gm_low[...] = gmr[...].astype(BF16)

    arrived(n1_copies)
    n1_next = post(n1c, n1p, at_seq(seq + 1))
    g2_copies = to_members(lambda t: g2r.at[:, cols(t)], g2h.at[rows(sub, 8)])
    gm_copies = to_members(lambda t: gm_low.at[:, cols(t)], gmh.at[rows(sub, 32)])
    g2h[rows(sub, 8), :] = g2r[:, cols(sub)]
    gmh[rows(sub, 32), :] = gm_low[:, cols(sub)]

    bias1 = jnp.where(seq > 0, 0.0, NEGATIVE_FILL).astype(F32)

    def gains(level, k):
        here = pl.ds(multiple(sub * COLS + k * HEAD, HEAD), HEAD)
        return qg[level : level + 1, here], kg[level : level + 1, here]

    n1_next.wait_recv()
    arrived(h1_copies)
    for k in range(4):
        here = pl.ds(k * HEAD, HEAD)
        probs, attended = head_forward(n1c[:, here], n1p[:, here], *gains(1, k), bias1)
        p1[k] = probs
        u1[:, here] = (h1[:, here].astype(F32) + attended).astype(BF16)
    h2 = (dot(pool_matrix(), u1[...]) * 0.25).astype(BF16).astype(F32)
    sq[...] = fold(h2 * h2)
    sq_copies = [post(sq, sq_in.at[k - 1], (seq, peer(k))) for k in range(1, MEMBERS)]

    def seq_peer(k):
        return lax.rem(in_unit + k, 4)

    arrived(g2_copies)
    gl2[...] = g2h[...].astype(BF16)

    def head_cols(k):
        return pl.ds(multiple(k * HEAD, HEAD), HEAD)

    gl2_copies = [
        post(gl2.at[:, head_cols(seq_peer(k))], gl2h.at[rows(in_unit, 32)], at_seq(unit_base + seq_peer(k)))
        for k in range(1, 4)
    ]
    gl2h[rows(in_unit, 32), :] = gl2[:, head_cols(in_unit)]

    arrived(sq_copies)
    total = jnp.sum(sq[...] + sq_in[0] + sq_in[1] + sq_in[2], axis=-1, keepdims=True)
    inv2 = lax.rsqrt(total / WIDTH + EPSILON)
    n2r[...] = (h2 * inv2).astype(BF16)
    n2_copies = [
        post(n2r.at[:, head_cols(seq_peer(k))], n2c.at[rows(in_unit, 32)], at_seq(unit_base + seq_peer(k)))
        for k in range(1, 4)
    ]
    n2_copies += [
        post(n2r.at[:, head_cols(seq_peer(k))], n2p.at[rows(in_unit, 32)], at_seq(unit_base + 4 + seq_peer(k)))
        for k in range(4)
    ]
    n2c[rows(in_unit, 32), :] = n2r[:, head_cols(in_unit)]

    arrived(gl2_copies)
    arrived(n2_copies)
    bias2 = jnp.where(unit_base > 0, 0.0, NEGATIVE_FILL).astype(F32)
    gains2 = gains(2, in_unit)
    probs2, attended2 = head_forward(n2c[...], n2p[...], *gains2, bias2)
    term_cur, term_prev = head_backward(n2c[...], n2p[...], *gains2, probs2, gl2h[...])
    c2[:, 0:HEAD] = attended2.astype(BF16)
    c2[:, HEAD : 2 * HEAD] = term_cur.astype(BF16)
    gp2[...] = term_prev.astype(BF16)
    c2_copies = [
        post(gp2.at[rows(seq_peer(k), 32)], r2p.at[in_unit], at_seq(unit_base - 4 + seq_peer(k)))
        for k in range(4)
    ]
    c2_copies += [
        post(c2.at[rows(seq_peer(k), 32)], r2c.at[in_unit], at_seq(unit_base + seq_peer(k)))
        for k in range(1, 4)
    ]
    r2c[in_unit] = c2[rows(in_unit, 32), :]

    arrived(c2_copies)
    unit2 = h2 * inv2
    term2 = jnp.concatenate(
        [r2c[k][:, HEAD : 2 * HEAD].astype(F32) + r2p[k].astype(F32) for k in range(4)], axis=1
    )
    dz[...] = fold(term2 * unit2)
    dz_copies = [post(dz, dz_in.at[k - 1], (seq, peer(k))) for k in range(1, MEMBERS)]
    attended2_rows = jnp.concatenate([r2c[k][:, 0:HEAD].astype(F32) for k in range(4)], axis=1)
    u2 = (h2 + attended2_rows).astype(BF16)
    u2x[0:32, :] = u2
    last2 = u2.astype(F32)[31:32]
    last1 = u1[ROWS - 16 :, :].astype(F32)[15:16] + last2
    row, _ = iotas(16, COLS)
    edge[...] = jnp.where(row == 0, last2, jnp.where(row == 1, last1, 0.0)).astype(BF16)
    edge_copy = post(edge, edge_in, at_seq(seq + 1))

    arrived(dz_copies)
    total = jnp.sum(dz[...] + dz_in[0] + dz_in[1] + dz_in[2], axis=-1, keepdims=True)
    back2 = g2h[...] + inv2 * (term2 - unit2 * (total / WIDTH))
    b2[...] = back2
    b2_copies = to_members(lambda t: b2.at[rows(t, 8)], b2r.at[:, cols(sub)])
    b2r[:, cols(sub)] = b2[rows(sub, 8), :]

    arrived(gm_copies)
    grad1 = gmh[...].astype(F32) + split_dot(repeat_matrix(), b2[...]) * 0.25
    gl1[...] = grad1.astype(BF16)
    back_copies = []
    for k in range(4):
        here = pl.ds(k * HEAD, HEAD)
        term_cur, term_prev = head_backward(
            n1c[:, here], n1p[:, here], *gains(1, k), p1[k], gl1[:, here]
        )
        gp1[k] = term_prev.astype(BF16)
        back_copies.append(post(gp1.at[k], gr1.at[k], at_seq(seq - 1)))
        gc1[:, here] = term_cur

    edge_copy.wait_recv()
    before = jnp.where(seq > 0, edge_in[...].astype(F32), 0.0)
    u2x[32:48, :] = before.astype(BF16)
    up = up_matrix()
    mid = (u1[...].astype(F32) + dot(up, u2x[...])).astype(BF16)
    mid_wide = mid.astype(F32)
    for j in range(MEMBERS):
        midx[j, 0:32, :] = mid[32 * j : 32 * (j + 1)]
        ahead = mid_wide[32 * j - 1 : 32 * j] if j > 0 else before[1:2]
        midx[j, 32:48, :] = jnp.broadcast_to(ahead, (16, COLS)).astype(BF16)

    for k in range(4):
        here = pl.ds(k * HEAD, HEAD)
        back_copies[k].wait_recv()
        g1s[:, here] = (gc1[:, here] + gr1[k].astype(F32)).astype(BF16)
    g1_copies = to_members(lambda t: g1s.at[rows(t, 32)], g1r.at[:, cols(sub)])
    mid_copies = to_members(lambda t: midx.at[t], midr.at[:, cols(sub)])
    g1r[:, cols(sub)] = g1s[rows(sub, 32), :]
    midr[:, cols(sub)] = midx[sub]

    arrived(b2_copies)
    repeat8 = repeat_matrix()[0:32, 0:8]
    arrived(g1_copies)
    unit1 = h1_rows * inv1
    term1 = g1r[...].astype(F32)
    along = jnp.sum(term1 * unit1, axis=-1, keepdims=True) / WIDTH
    back1 = gmr[...] + split_dot(repeat8, b2r[...]) * 0.25 + inv1 * (term1 - unit1 * along)
    gmr[...] = back1

    back_index = take(4)

    def back_halo(chunk):
        here = cols(chunk)
        return remote(gp0.at[:, here], gr0.at[:, here], back_index + chunk, at_device(device - 1))

    def backward_chunk(chunk, _):
        wide = cols(chunk)
        grad = cotx[0:ROWS, wide].astype(F32) + split_dot(repeat_matrix(), gmr[:, wide]) * 0.25
        g0[:, wide] = grad
        gl0[...] = grad.astype(BF16)
        for k in range(4):
            here = pl.ds(multiple(chunk * COLS + k * HEAD, HEAD), HEAD)
            term_cur, term_prev = head_backward(
                n0[:, here], n0p[:, here], qg[0:1, here], kg[0:1, here],
                p0[chunk * 4 + k], gl0[:, k * HEAD : (k + 1) * HEAD],
            )
            gp0[:, here] = term_prev.astype(BF16)
            gc0[:, here] = term_cur
        back_halo(chunk).start()
        return 0

    lax.fori_loop(0, 4, backward_chunk, 0)

    arrived(mid_copies)

    def output_chunk(chunk, _):
        here = cols(chunk)
        out_v[:, here] = (u0[:, here].astype(F32) + dot(up_matrix(), midr[:, here])).astype(BF16)
        return 0

    lax.fori_loop(0, 4, output_chunk, 0)
    store_out = pltpu.make_async_copy(out_v, out_hbm, local_sem.at[2])
    store_out.start()

    for chunk in range(4):
        back_halo(chunk).wait_recv()

    def finish_rows(block, _):
        here = pl.ds(multiple(block * 16, 16), 16)
        inv = inv0[here, :]
        unit = tok[here, :].astype(F32) * inv
        term = gc0[here, :] + gr0[here, :].astype(F32)
        along = jnp.sum(term * unit, axis=-1, keepdims=True) / WIDTH
        u0[here, :] = (g0[here, :] + inv * (term - unit * along)).astype(BF16)
        return 0

    lax.fori_loop(0, ROWS // 16, finish_rows, 0)
    store_grad = pltpu.make_async_copy(u0, grad_hbm, local_sem.at[3])
    store_grad.start()
    for copy in sent:
        copy.wait_send()
    for chunk in range(4):
        halo(chunk).wait_send()
        back_halo(chunk).wait_send()
    store_out.wait()
    store_grad.wait()


def per_device(tokens, cotangent, query_gain, key_gain):
    groups = lax.axis_size("seq")
    shape = jax.ShapeDtypeStruct(tokens.shape, BF16)

    def low(*extent):
        return pltpu.VMEM(extent, BF16)

    def wide(*extent):
        return pltpu.VMEM(extent, F32)

    rows_low = low(ROWS, WIDTH)
    scratch = dict(
        tok=rows_low, cotx=low(ROWS + 16, WIDTH), n0=rows_low, n0p=rows_low, u0=rows_low,
        p0=wide(HEADS, ROWS, ROWS), inv0=wide(ROWS, 1), gc0=wide(ROWS, WIDTH), gp0=rows_low,
        gr0=rows_low, g0=wide(ROWS, WIDTH), out_v=rows_low,
        h1r=low(32, WIDTH), n1r=low(32, WIDTH), n1c=low(ROWS, COLS), n1p=low(ROWS, COLS),
        h1=low(ROWS, COLS), p1=wide(4, ROWS, ROWS), u1=low(ROWS, COLS), u1_in=low(32, WIDTH),
        gmr=wide(32, WIDTH), g2r=wide(8, WIDTH), gmh=low(ROWS, COLS), g2h=wide(32, COLS),
        sq=wide(32, HEAD), sq_in=wide(3, 32, HEAD), n2r=low(32, COLS), n2c=low(ROWS, HEAD),
        n2p=low(ROWS, HEAD), gl2=low(32, COLS), gl2h=low(ROWS, HEAD), c2=low(ROWS, 2 * HEAD),
        gp2=low(ROWS, HEAD), r2c=low(4, 32, 2 * HEAD), r2p=low(4, 32, HEAD), dz=wide(32, HEAD),
        dz_in=wide(3, 32, HEAD), u2x=low(48, COLS), edge=low(16, COLS), edge_in=low(16, COLS),
        midx=low(4, 48, COLS), midr=low(48, WIDTH), b2=wide(32, COLS), b2r=wide(8, WIDTH),
        gl1=low(ROWS, COLS), gc1=wide(ROWS, COLS), gp1=low(4, ROWS, HEAD), gr1=low(4, ROWS, HEAD),
        g1s=low(ROWS, COLS), g1r=low(32, WIDTH), gl0=low(ROWS, COLS),
    )
    hbm = pl.BlockSpec(memory_space=pl.ANY)
    vmem = pl.BlockSpec(memory_space=pltpu.VMEM)

    def body(*refs):
        kernel(groups, *refs)

    return pl.pallas_call(
        body,
        out_shape=(shape, shape),
        in_specs=[hbm, hbm, vmem, vmem],
        out_specs=(hbm, hbm),
        scratch_shapes=list(scratch.values())
        + [
            pltpu.SemaphoreType.DMA((4,)),
            pltpu.SemaphoreType.DMA((72,)),
            pltpu.SemaphoreType.DMA((72,)),
        ],
        compiler_params=pltpu.CompilerParams(
            collective_id=0, has_side_effects=True, vmem_limit_bytes=48 * 2**20
        ),
    )(tokens, cotangent, query_gain, key_gain)


def solution(mesh):
    placed = (P(("seq", "sub"), None), P(("seq", "sub"), None), P(), P())
    return jax.shard_map(
        per_device,
        mesh=mesh,
        in_specs=placed,
        out_specs=(P(("seq", "sub"), None), P(("seq", "sub"), None)),
        check_vma=False,
    )
```

time: 365 us -> 99.5 us (0.27)
  the two profiles are of different devices: /device:TPU:1 before, /device:TPU:128 now
where the time goes in v1:
time: 99.5 us; the launch traced here: 99.2 us
  Pallas kernels  93.4 us (94%)
  local copies, waits for them, and re-layouts  5.18 us (5%)
    pallas_call x1, Pallas kernels, per_device(): pl.pallas_call(body, out_shape=(shape, shape), in_specs=[hbm, hbm, vmem,...  93.4 us
    unnamed x10, local copies, waits for them, and re-layouts  5.18 us

profile of v1, /device:TPU:128, one launch (start us, length us, event | category | flops | bytes accessed | tf_op | source)
XLA Modules:
  0.0 99.2 jit_solution(6726666118979736018)
XLA Ops:
  0.6 0.0 copy-start
  0.6 1.0 %copy-done = bf16[128,2048]{1,0:T(8,128)(2,1)S(1)} copy-done((bf16[128,2048]{1,0:T(8,128)(2,1)S(1)}, bf16[128,2048]{1,0:T(8,128)(2,1)}, u32[]{:S(2)}) %copy-start) | copy-done | bytes 524312
  1.7 0.0 copy-start.1
  1.7 1.0 %copy-done.1 = bf16[128,2048]{1,0:T(8,128)(2,1)S(1)} copy-done((bf16[128,2048]{1,0:T(8,128)(2,1)S(1)}, bf16[128,2048]{1,0:T(8,128)(2,1)}, u32[]{:S(2)}) %copy-start.1) | copy-done | bytes 524312
  2.7 0.0 copy-start.2
  2.7 0.8 copy-done.2
  3.5 0.0 copy-start.3
  3.5 0.8 copy-done.3
  4.2 93.4 %shard_map.59 = (bf16[128,2048]{1,0:T(8,128)(2,1)S(1)}, bf16[128,2048]{1,0:T(8,128)(2,1)S(1)}) custom-call(bf16[128,2048]{1,0:T(8,128)(2,1)S(1)} %copy-done, bf16[128,2048]{1,0:T(8,128)(2,1)S(1)} %copy-done.1, f32[3,2048]{1,0:T(4,128)S(1)} %copy-done.2, f32[3,2048]{1,0:T(4,128)S(1)} %copy-done.3), custom_call_target="tpu_custom_call" | custom-call | tf_op jit(solution)/shard_map/pallas_call | solution.py:479
  97.6 0.8 copy.8
  98.4 0.8 copy.9
Async XLA Ops:
  0.6 1.0 %copy-start = (bf16[128,2048]{1,0:T(8,128)(2,1)S(1)}, bf16[128,2048]{1,0:T(8,128)(2,1)}, u32[]{:S(2)}) copy-start(bf16[128,2048]{1,0:T(8,128)(2,1)} %refs_0_.1) | copy-start | bytes 1572868
  1.7 1.0 %copy-start.1 = (bf16[128,2048]{1,0:T(8,128)(2,1)S(1)}, bf16[128,2048]{1,0:T(8,128)(2,1)}, u32[]{:S(2)}) copy-start(bf16[128,2048]{1,0:T(8,128)(2,1)} %refs_1_.1) | copy-start | bytes 1572868
  2.7 0.8 copy-start.2
  3.5 0.8 copy-start.3

commit v2 on v1

--- a/solution.py
+++ b/solution.py
@@ -58,43 +58,62 @@
     return (normed.astype(F32) * gain).astype(BF16)
 
 
-def head_forward(cur, prev, query_gain, key_gain, prev_bias):
+def forward_heads(heads, prev_bias):
     own = own_mask()
-    query = gained(cur, query_gain)
     scale = HEAD ** (-0.5)
-    scores = jnp.where(
-        own,
-        dot_t(query, gained(cur, key_gain)) * scale,
-        dot_t(query, gained(prev, key_gain)) * scale + prev_bias,
-    )
-    weights = jnp.exp(scores - jnp.max(scores, axis=-1, keepdims=True))
-    probs = weights / jnp.sum(weights, axis=-1, keepdims=True)
-    zero = jnp.zeros_like(probs)
-    attended = dot(jnp.where(own, probs, zero).astype(BF16), cur) + dot(
-        jnp.where(own, zero, probs).astype(BF16), prev
-    )
-    return probs, attended
-
-
-def head_backward(cur, prev, query_gain, key_gain, probs, grad):
+    queries = [gained(cur, qg) for cur, _, qg, _ in heads]
+    near = [dot_t(q, gained(h[0], h[3])) for q, h in zip(queries, heads)]
+    far = [dot_t(q, gained(h[1], h[3])) for q, h in zip(queries, heads)]
+    scores = [jnp.where(own, a * scale, b * scale + prev_bias) for a, b in zip(near, far)]
+    tops = [jnp.max(s, axis=-1, keepdims=True) for s in scores]
+    weights = [jnp.exp(s - t) for s, t in zip(scores, tops)]
+    sums = [jnp.sum(w, axis=-1, keepdims=True) for w in weights]
+    probs = [w / s for w, s in zip(weights, sums)]
+    low = [p.astype(BF16) for p in probs]
+    zero = jnp.zeros((ROWS, ROWS), BF16)
+    attended = [
+        dot(jnp.where(own, p, zero), h[0]) + dot(jnp.where(own, zero, p), h[1])
+        for p, h in zip(low, heads)
+    ]
+    return list(zip(probs, attended))
+
+
+def backward_heads(heads):
     own = own_mask()
-    query = gained(cur, query_gain)
-    zero = jnp.zeros_like(probs)
-    d_probs = jnp.where(own, dot_t(grad, cur), dot_t(grad, prev))
-    center = jnp.sum(probs * d_probs, axis=-1, keepdims=True)
-    d_scores = probs * (d_probs - center) * HEAD ** (-0.5)
-    ds_cur = jnp.where(own, d_scores, zero).astype(BF16)
-    ds_prev = jnp.where(own, zero, d_scores).astype(BF16)
-    p_cur = jnp.where(own, probs, zero).astype(BF16)
-    p_prev = jnp.where(own, zero, probs).astype(BF16)
-    d_query = dot(ds_cur, gained(cur, key_gain)) + dot(ds_prev, gained(prev, key_gain))
-    term_cur = d_query * query_gain + t_dot(ds_cur, query) * key_gain + t_dot(p_cur, grad)
-    term_prev = t_dot(ds_prev, query) * key_gain + t_dot(p_prev, grad)
-    return term_cur, term_prev
-
-
-def fold(x):
-    return sum(x[:, HEAD * k : HEAD * (k + 1)] for k in range(COLS // HEAD))
+    zero = jnp.zeros((ROWS, ROWS), BF16)
+    queries = [gained(h[0], h[2]) for h in heads]
+    d_probs = [jnp.where(own, dot_t(h[5], h[0]), dot_t(h[5], h[1])) for h in heads]
+    low = [h[4].astype(BF16) for h in heads]
+    v_cur = [t_dot(jnp.where(own, p, zero), h[5]) for p, h in zip(low, heads)]
+    v_prev = [t_dot(jnp.where(own, zero, p), h[5]) for p, h in zip(low, heads)]
+    centers = [jnp.sum(h[4] * d, axis=-1, keepdims=True) for h, d in zip(heads, d_probs)]
+    d_scores = [
+        (h[4] * (d - c) * HEAD ** (-0.5)).astype(BF16) for h, d, c in zip(heads, d_probs, centers)
+    ]
+    ds_cur = [jnp.where(own, d, zero) for d in d_scores]
+    ds_prev = [jnp.where(own, zero, d) for d in d_scores]
+    k_prev = [t_dot(d, q) for d, q in zip(ds_prev, queries)]
+    k_cur = [t_dot(d, q) for d, q in zip(ds_cur, queries)]
+    d_query = [
+        dot(a, gained(h[0], h[3])) + dot(b, gained(h[1], h[3]))
+        for a, b, h in zip(ds_cur, ds_prev, heads)
+    ]
+    return [
+        (dq * h[2] + kc * h[3] + vc, kp * h[3] + vp)
+        for h, dq, kc, vc, kp, vp in zip(heads, d_query, k_cur, v_cur, k_prev, v_prev)
+    ]
+
+
+def packed(column):
+    row, col = iotas(32, HEAD)
+    line = jnp.sum(jnp.where(row == col, column, 0.0), axis=0, keepdims=True)
+    return jnp.broadcast_to(line, (8, HEAD))
+
+
+def unpacked(tile):
+    row, col = iotas(32, HEAD)
+    line = jnp.broadcast_to(tile[0:1], (32, HEAD))
+    return jnp.sum(jnp.where(row == col, line, 0.0), axis=-1, keepdims=True)
 
 
 def up_matrix():
@@ -114,11 +133,11 @@
 
 
 def kernel(
-    groups, tokens_hbm, cot_hbm, qg, kg, out_hbm, grad_hbm,
-    tok, cotx, n0, n0p, u0, p0, inv0, gc0, gp0, gr0, g0, out_v,
-    h1r, n1r, n1c, n1p, h1, p1, u1, u1_in, gmr, g2r, gmh, g2h,
+    groups, tokens_hbm, cot_hbm, qg_hbm, kg_hbm, out_v, grad_out,
+    qg, kg, tok, cotx, n0, n0p, u0, p0, inv0, weight0, gc0, gp0, gr0, g0,
+    h1r, n1r, n1c, n1p, h1, p1, u1, gm_low, gmr, g2r, gmh, g2h,
     sq, sq_in, n2r, n2c, n2p, gl2, gl2h, c2, gp2, r2c, r2p, dz, dz_in,
-    u2x, edge, edge_in, midx, midr, b2, b2r, gl1, gc1, gp1, gr1, g1s, g1r, gl0,
+    u1r, u2s, u2r, mid, edge, edge_in, b2, b2r, gl1, gc1, gp1, gr1, g1s, g1r,
     local_sem, send_sem, recv_sem,
 ):
     seq = lax.axis_index("seq")
@@ -172,7 +191,11 @@
 
     load_tok = pltpu.make_async_copy(tokens_hbm, tok, local_sem.at[0])
     load_cot = pltpu.make_async_copy(cot_hbm, cotx.at[pl.ds(0, ROWS)], local_sem.at[1])
+    load_qg = pltpu.make_async_copy(qg_hbm, qg, local_sem.at[2])
+    load_kg = pltpu.make_async_copy(kg_hbm, kg, local_sem.at[3])
     load_tok.start()
+    load_qg.start()
+    load_kg.start()
     load_cot.start()
     barrier = pltpu.get_barrier_semaphore()
     partners = [at_device(device + 1), at_device(device - 1)]
@@ -209,17 +232,19 @@
         cotx.at[pl.ds(0, 16)], cotx.at[pl.ds(ROWS, 16)], at_device(device - 1)
     )
 
+    load_qg.wait()
+    load_kg.wait()
     bias0 = jnp.where(device > 0, 0.0, NEGATIVE_FILL).astype(F32)
 
     def forward_chunk(chunk, _):
         halo(chunk).wait_recv()
-        for k in range(4):
-            here = pl.ds(multiple(chunk * COLS + k * HEAD, HEAD), HEAD)
-            probs, attended = head_forward(
-                n0[:, here], n0p[:, here], qg[0:1, here], kg[0:1, here], bias0
-            )
+        spans = [pl.ds(multiple(chunk * COLS + k * HEAD, HEAD), HEAD) for k in range(4)]
+        results = forward_heads(
+            [(n0[:, here], n0p[:, here], qg[0:1, here], kg[0:1, here]) for here in spans], bias0
+        )
+        for k, (probs, attended) in enumerate(results):
             p0[chunk * 4 + k] = probs
-            u0[:, here] = (tok[:, here].astype(F32) + attended).astype(BF16)
+            u0[:, spans[k]] = (tok[:, spans[k]].astype(F32) + attended).astype(BF16)
         h1r[:, cols(chunk)] = (dot(pool_matrix(), u0[:, cols(chunk)]) * 0.25).astype(BF16)
         return 0
 
@@ -245,7 +270,6 @@
         summed = dot(gather, cotx[:, here])
         gmr[:, here] = summed[0:32]
         g2r[:, here] = summed[32:40]
-    gm_low = u1_in
     gm_low[...] = gmr[...].astype(BF16)
 
     arrived(n1_copies)
@@ -262,14 +286,16 @@
         return qg[level : level + 1, here], kg[level : level + 1, here]
 
     n1_next.wait_recv()
+    spans = [pl.ds(k * HEAD, HEAD) for k in range(4)]
+    results = forward_heads(
+        [(n1c[:, here], n1p[:, here], *gains(1, k)) for k, here in enumerate(spans)], bias1
+    )
     arrived(h1_copies)
-    for k in range(4):
-        here = pl.ds(k * HEAD, HEAD)
-        probs, attended = head_forward(n1c[:, here], n1p[:, here], *gains(1, k), bias1)
+    for k, (probs, attended) in enumerate(results):
         p1[k] = probs
-        u1[:, here] = (h1[:, here].astype(F32) + attended).astype(BF16)
+        u1[:, spans[k]] = (h1[:, spans[k]].astype(F32) + attended).astype(BF16)
     h2 = (dot(pool_matrix(), u1[...]) * 0.25).astype(BF16).astype(F32)
-    sq[...] = fold(h2 * h2)
+    sq[...] = packed(jnp.sum(h2 * h2, axis=-1, keepdims=True))
     sq_copies = [post(sq, sq_in.at[k - 1], (seq, peer(k))) for k in range(1, MEMBERS)]
 
     def seq_peer(k):
@@ -288,7 +314,7 @@
     gl2h[rows(in_unit, 32), :] = gl2[:, head_cols(in_unit)]
 
     arrived(sq_copies)
-    total = jnp.sum(sq[...] + sq_in[0] + sq_in[1] + sq_in[2], axis=-1, keepdims=True)
+    total = unpacked(sq[...] + sq_in[0] + sq_in[1] + sq_in[2])
     inv2 = lax.rsqrt(total / WIDTH + EPSILON)
     n2r[...] = (h2 * inv2).astype(BF16)
     n2_copies = [
@@ -301,12 +327,15 @@
     ]
     n2c[rows(in_unit, 32), :] = n2r[:, head_cols(in_unit)]
 
+    u1_copies = to_members(lambda t: u1.at[rows(t, 32)], u1r.at[:, cols(sub)])
+    u1r[:, cols(sub)] = u1[rows(sub, 32), :]
+
     arrived(gl2_copies)
     arrived(n2_copies)
     bias2 = jnp.where(unit_base > 0, 0.0, NEGATIVE_FILL).astype(F32)
     gains2 = gains(2, in_unit)
-    probs2, attended2 = head_forward(n2c[...], n2p[...], *gains2, bias2)
-    term_cur, term_prev = head_backward(n2c[...], n2p[...], *gains2, probs2, gl2h[...])
+    ((probs2, attended2),) = forward_heads([(n2c[...], n2p[...], *gains2)], bias2)
+    ((term_cur, term_prev),) = backward_heads([(n2c[...], n2p[...], *gains2, probs2, gl2h[...])])
     c2[:, 0:HEAD] = attended2.astype(BF16)
     c2[:, HEAD : 2 * HEAD] = term_cur.astype(BF16)
     gp2[...] = term_prev.astype(BF16)
@@ -325,19 +354,23 @@
     term2 = jnp.concatenate(
         [r2c[k][:, HEAD : 2 * HEAD].astype(F32) + r2p[k].astype(F32) for k in range(4)], axis=1
     )
-    dz[...] = fold(term2 * unit2)
+    dz[...] = packed(jnp.sum(term2 * unit2, axis=-1, keepdims=True))
     dz_copies = [post(dz, dz_in.at[k - 1], (seq, peer(k))) for k in range(1, MEMBERS)]
     attended2_rows = jnp.concatenate([r2c[k][:, 0:HEAD].astype(F32) for k in range(4)], axis=1)
     u2 = (h2 + attended2_rows).astype(BF16)
-    u2x[0:32, :] = u2
-    last2 = u2.astype(F32)[31:32]
-    last1 = u1[ROWS - 16 :, :].astype(F32)[15:16] + last2
+    u2_wide = u2.astype(F32)
     row, _ = iotas(16, COLS)
-    edge[...] = jnp.where(row == 0, last2, jnp.where(row == 1, last1, 0.0)).astype(BF16)
+
+    def u1_row(r):
+        return u1[r - 15 : r + 1, :].astype(F32)[15:16]
+
+    edge[...] = jnp.where(
+        row == 0, u2_wide[31:32], jnp.where(row == 1, u1_row(ROWS - 1), 0.0)
+    ).astype(BF16)
     edge_copy = post(edge, edge_in, at_seq(seq + 1))
 
     arrived(dz_copies)
-    total = jnp.sum(dz[...] + dz_in[0] + dz_in[1] + dz_in[2], axis=-1, keepdims=True)
+    total = unpacked(dz[...] + dz_in[0] + dz_in[1] + dz_in[2])
     back2 = g2h[...] + inv2 * (term2 - unit2 * (total / WIDTH))
     b2[...] = back2
     b2_copies = to_members(lambda t: b2.at[rows(t, 8)], b2r.at[:, cols(sub)])
@@ -347,34 +380,36 @@
     grad1 = gmh[...].astype(F32) + split_dot(repeat_matrix(), b2[...]) * 0.25
     gl1[...] = grad1.astype(BF16)
     back_copies = []
-    for k in range(4):
-        here = pl.ds(k * HEAD, HEAD)
-        term_cur, term_prev = head_backward(
-            n1c[:, here], n1p[:, here], *gains(1, k), p1[k], gl1[:, here]
-        )
+    results = backward_heads(
+        [
+            (n1c[:, here], n1p[:, here], *gains(1, k), p1[k], gl1[:, here])
+            for k, here in enumerate(spans)
+        ]
+    )
+    for k, (term_cur, term_prev) in enumerate(results):
         gp1[k] = term_prev.astype(BF16)
         back_copies.append(post(gp1.at[k], gr1.at[k], at_seq(seq - 1)))
-        gc1[:, here] = term_cur
+        gc1[:, spans[k]] = term_cur
 
     edge_copy.wait_recv()
-    before = jnp.where(seq > 0, edge_in[...].astype(F32), 0.0)
-    u2x[32:48, :] = before.astype(BF16)
-    up = up_matrix()
-    mid = (u1[...].astype(F32) + dot(up, u2x[...])).astype(BF16)
-    mid_wide = mid.astype(F32)
-    for j in range(MEMBERS):
-        midx[j, 0:32, :] = mid[32 * j : 32 * (j + 1)]
-        ahead = mid_wide[32 * j - 1 : 32 * j] if j > 0 else before[1:2]
-        midx[j, 32:48, :] = jnp.broadcast_to(ahead, (16, COLS)).astype(BF16)
+    before = edge_in[...].astype(F32)
+    row, _ = iotas(8, COLS)
+    for t in range(MEMBERS):
+        if t == 0:
+            coarse, fine = before[0:1], before[1:2]
+        else:
+            coarse, fine = u2_wide[8 * t - 1 : 8 * t], u1_row(32 * t - 1)
+        tail = jnp.where(row == 0, coarse, jnp.where(row == 1, fine, 0.0))
+        u2s[t] = jnp.concatenate([u2_wide[8 * t : 8 * t + 8], tail], axis=0).astype(BF16)
+    u2_copies = to_members(lambda t: u2s.at[t], u2r.at[:, cols(sub)])
+    u2r[:, cols(sub)] = u2s[sub]
 
     for k in range(4):
         here = pl.ds(k * HEAD, HEAD)
         back_copies[k].wait_recv()
         g1s[:, here] = (gc1[:, here] + gr1[k].astype(F32)).astype(BF16)
     g1_copies = to_members(lambda t: g1s.at[rows(t, 32)], g1r.at[:, cols(sub)])
-    mid_copies = to_members(lambda t: midx.at[t], midr.at[:, cols(sub)])
     g1r[:, cols(sub)] = g1s[rows(sub, 32), :]
-    midr[:, cols(sub)] = midx[sub]
 
     arrived(b2_copies)
     repeat8 = repeat_matrix()[0:32, 0:8]
@@ -395,53 +430,66 @@
         wide = cols(chunk)
         grad = cotx[0:ROWS, wide].astype(F32) + split_dot(repeat_matrix(), gmr[:, wide]) * 0.25
         g0[:, wide] = grad
-        gl0[...] = grad.astype(BF16)
-        for k in range(4):
-            here = pl.ds(multiple(chunk * COLS + k * HEAD, HEAD), HEAD)
-            term_cur, term_prev = head_backward(
-                n0[:, here], n0p[:, here], qg[0:1, here], kg[0:1, here],
-                p0[chunk * 4 + k], gl0[:, k * HEAD : (k + 1) * HEAD],
-            )
+        spans = [pl.ds(multiple(chunk * COLS + k * HEAD, HEAD), HEAD) for k in range(4)]
+        low = grad.astype(BF16)
+        results = backward_heads(
+            [
+                (n0[:, here], n0p[:, here], qg[0:1, here], kg[0:1, here],
+                 p0[chunk * 4 + k], low[:, k * HEAD : (k + 1) * HEAD])
+                for k, here in enumerate(spans)
+            ]
+        )
+        for here, (_, term_prev) in zip(spans, results):
             gp0[:, here] = term_prev.astype(BF16)
+        back_halo(chunk).start()
+        for here, (term_cur, _) in zip(spans, results):
             gc0[:, here] = term_cur
-        back_halo(chunk).start()
         return 0
 
     lax.fori_loop(0, 4, backward_chunk, 0)
 
-    arrived(mid_copies)
+    arrived(u1_copies)
+    arrived(u2_copies)
+    row, col = iotas(32, 16)
+    inside = (col < 8) & (row >= 4 * col + 3) & (row <= 4 * col + 6)
+    lift = ones_where(inside | ((col == 8) & (row <= 2) & (device > 0)))
 
     def output_chunk(chunk, _):
         here = cols(chunk)
-        out_v[:, here] = (u0[:, here].astype(F32) + dot(up_matrix(), midr[:, here])).astype(BF16)
+        coarse = u2r[:, here]
+        mid[0:32, here] = (u1r[:, here].astype(F32) + dot(lift, coarse)).astype(BF16)
+        last = coarse.astype(F32)
+        last = jnp.where(device > 0, last[8:9] + last[9:10], 0.0)
+        mid[32:48, here] = jnp.broadcast_to(last, (16, COLS)).astype(BF16)
+        out_v[:, here] = (u0[:, here].astype(F32) + dot(up_matrix(), mid[:, here])).astype(BF16)
         return 0
 
     lax.fori_loop(0, 4, output_chunk, 0)
-    store_out = pltpu.make_async_copy(out_v, out_hbm, local_sem.at[2])
-    store_out.start()
-
-    for chunk in range(4):
+
+    inv = inv0[...]
+
+    def term_chunk(chunk, along):
+        here = cols(chunk)
         back_halo(chunk).wait_recv()
+        term = gc0[:, here] + gr0[:, here].astype(F32)
+        g0[:, here] = g0[:, here] + inv * term
+        part = term * tok[:, here].astype(F32)
+        return along + sum(part[:, k * HEAD : (k + 1) * HEAD] for k in range(COLS // HEAD))
+
+    along = lax.fori_loop(0, 4, term_chunk, jnp.zeros((ROWS, HEAD), F32))
+    weight0[...] = inv * inv * inv * (jnp.sum(along, axis=-1, keepdims=True) / WIDTH)
 
     def finish_rows(block, _):
         here = pl.ds(multiple(block * 16, 16), 16)
-        inv = inv0[here, :]
-        unit = tok[here, :].astype(F32) * inv
-        term = gc0[here, :] + gr0[here, :].astype(F32)
-        along = jnp.sum(term * unit, axis=-1, keepdims=True) / WIDTH
-        u0[here, :] = (g0[here, :] + inv * (term - unit * along)).astype(BF16)
+        grad_out[here, :] = (g0[here, :] - weight0[here, :] * tok[here, :].astype(F32)).astype(BF16)
         return 0
 
     lax.fori_loop(0, ROWS // 16, finish_rows, 0)
-    store_grad = pltpu.make_async_copy(u0, grad_hbm, local_sem.at[3])
-    store_grad.start()
     for copy in sent:
         copy.wait_send()
     for chunk in range(4):
         halo(chunk).wait_send()
         back_halo(chunk).wait_send()
-    store_out.wait()
-    store_grad.wait()
 
 
 def per_device(tokens, cotangent, query_gain, key_gain):
@@ -456,21 +504,22 @@
 
     rows_low = low(ROWS, WIDTH)
     scratch = dict(
-        tok=rows_low, cotx=low(ROWS + 16, WIDTH), n0=rows_low, n0p=rows_low, u0=rows_low,
-        p0=wide(HEADS, ROWS, ROWS), inv0=wide(ROWS, 1), gc0=wide(ROWS, WIDTH), gp0=rows_low,
-        gr0=rows_low, g0=wide(ROWS, WIDTH), out_v=rows_low,
+        qg=wide(3, WIDTH), kg=wide(3, WIDTH), tok=rows_low, cotx=low(ROWS + 16, WIDTH), n0=rows_low, n0p=rows_low, u0=rows_low,
+        p0=wide(HEADS, ROWS, ROWS), inv0=wide(ROWS, 1), weight0=wide(ROWS, 1), gc0=wide(ROWS, WIDTH), gp0=rows_low,
+        gr0=rows_low, g0=wide(ROWS, WIDTH),
         h1r=low(32, WIDTH), n1r=low(32, WIDTH), n1c=low(ROWS, COLS), n1p=low(ROWS, COLS),
-        h1=low(ROWS, COLS), p1=wide(4, ROWS, ROWS), u1=low(ROWS, COLS), u1_in=low(32, WIDTH),
+        h1=low(ROWS, COLS), p1=wide(4, ROWS, ROWS), u1=low(ROWS, COLS), gm_low=low(32, WIDTH),
         gmr=wide(32, WIDTH), g2r=wide(8, WIDTH), gmh=low(ROWS, COLS), g2h=wide(32, COLS),
-        sq=wide(32, HEAD), sq_in=wide(3, 32, HEAD), n2r=low(32, COLS), n2c=low(ROWS, HEAD),
+        sq=wide(8, HEAD), sq_in=wide(3, 8, HEAD), n2r=low(32, COLS), n2c=low(ROWS, HEAD),
         n2p=low(ROWS, HEAD), gl2=low(32, COLS), gl2h=low(ROWS, HEAD), c2=low(ROWS, 2 * HEAD),
-        gp2=low(ROWS, HEAD), r2c=low(4, 32, 2 * HEAD), r2p=low(4, 32, HEAD), dz=wide(32, HEAD),
-        dz_in=wide(3, 32, HEAD), u2x=low(48, COLS), edge=low(16, COLS), edge_in=low(16, COLS),
-        midx=low(4, 48, COLS), midr=low(48, WIDTH), b2=wide(32, COLS), b2r=wide(8, WIDTH),
+        gp2=low(ROWS, HEAD), r2c=low(4, 32, 2 * HEAD), r2p=low(4, 32, HEAD), dz=wide(8, HEAD),
+        dz_in=wide(3, 8, HEAD), u1r=low(32, WIDTH), u2s=low(4, 16, COLS), u2r=low(16, WIDTH), mid=low(48, WIDTH), edge=low(16, COLS), edge_in=low(16, COLS),
+        b2=wide(32, COLS), b2r=wide(8, WIDTH),
         gl1=low(ROWS, COLS), gc1=wide(ROWS, COLS), gp1=low(4, ROWS, HEAD), gr1=low(4, ROWS, HEAD),
-        g1s=low(ROWS, COLS), g1r=low(32, WIDTH), gl0=low(ROWS, COLS),
+        g1s=low(ROWS, COLS), g1r=low(32, WIDTH),
     )
     hbm = pl.BlockSpec(memory_space=pl.ANY)
+
     vmem = pl.BlockSpec(memory_space=pltpu.VMEM)
 
     def body(*refs):
@@ -479,8 +528,8 @@
     return pl.pallas_call(
         body,
         out_shape=(shape, shape),
-        in_specs=[hbm, hbm, vmem, vmem],
-        out_specs=(hbm, hbm),
+        in_specs=[hbm] * 4,
+        out_specs=(vmem, vmem),
         scratch_shapes=list(scratch.values())
         + [
             pltpu.SemaphoreType.DMA((4,)),
@@ -488,7 +537,7 @@
             pltpu.SemaphoreType.DMA((72,)),
         ],
         compiler_params=pltpu.CompilerParams(
-            collective_id=0, has_side_effects=True, vmem_limit_bytes=48 * 2**20
+            collective_id=0, has_side_effects=True, vmem_limit_bytes=int(52.5 * 2**20)
         ),
     )(tokens, cotangent, query_gain, key_gain)
 

time: 99.5 us -> 91.6 us (0.921)
  the two profiles are of different devices: /device:TPU:128 before, /device:TPU:64 now
where the time goes in v2:
time: 91.6 us; the launch traced here: 91.3 us
  Pallas kernels  87.5 us (96%)
  local copies, waits for them, and re-layouts  3.1 us (3%)
    pallas_call x1, Pallas kernels, per_device(): pl.pallas_call(body, out_shape=(shape, shape), in_specs=[hbm] * 4, out_sp...  87.5 us
    unnamed x6, local copies, waits for them, and re-layouts  3.1 us

profile of v2, /device:TPU:64, one launch (start us, length us, event | category | flops | bytes accessed | tf_op | source)
XLA Modules:
  0.0 91.3 jit_solution(3869514240964187986)
XLA Ops:
  0.6 0.0 copy-start
  0.6 0.7 copy-done
  1.4 0.0 copy-start.1
  1.4 0.8 copy-done.1
  2.1 87.5 %shard_map.59 = (bf16[128,2048]{1,0:T(8,128)(2,1)S(1)}, bf16[128,2048]{1,0:T(8,128)(2,1)S(1)}) custom-call(bf16[128,2048]{1,0:T(8,128)(2,1)} %refs_0_.1, bf16[128,2048]{1,0:T(8,128)(2,1)} %refs_1_.1, f32[3,2048]{1,0:T(4,128)S(1)} %copy-done, f32[3,2048]{1,0:T(4,128)S(1)} %copy-done.1), custom_call_target="tpu_custom_call" | custom-call | tf_op jit(solution)/shard_map/pallas_call | solution.py:528
  89.7 0.8 copy.8
  90.5 0.8 copy.9
Async XLA Ops:
  0.6 0.8 copy-start
  1.4 0.8 copy-start.1

commit v3 on v2

--- a/solution.py
+++ b/solution.py
@@ -132,6 +132,32 @@
     return ones_where((col >= 4 * row) & (col < 4 * row + 4))
 
 
+class Guarded:
+    def __init__(self, copy, sends, takes, blank=None):
+        self.copy, self.sends, self.takes, self.blank = copy, sends, takes, blank
+
+    def start(self):
+        @pl.when(self.sends)
+        def _():
+            self.copy.start()
+
+    def wait_recv(self):
+        @pl.when(self.takes)
+        def _():
+            self.copy.wait_recv()
+
+        if self.blank is not None:
+
+            @pl.when(jnp.logical_not(self.takes))
+            def _():
+                self.blank[...] = jnp.zeros(self.blank.shape, self.blank.dtype)
+
+    def wait_send(self):
+        @pl.when(self.sends)
+        def _():
+            self.copy.wait_send()
+
+
 def kernel(
     groups, tokens_hbm, cot_hbm, qg_hbm, kg_hbm, out_v, grad_out,
     qg, kg, tok, cotx, n0, n0p, u0, p0, inv0, weight0, gc0, gp0, gr0, g0,
@@ -147,6 +173,11 @@
     in_unit = lax.rem(seq, 4)
     unit_base = seq - in_unit
 
+    first_device, last_device = device == 0, device == devices - 1
+    first_group, last_group = seq == 0, seq == groups - 1
+    first_unit, last_unit = unit_base == 0, unit_base == groups - 4
+    no = jnp.logical_not
+
     def at_seq(s):
         return (lax.rem(s + groups, groups), sub)
 
@@ -172,6 +203,12 @@
 
     def post(src, dst, target):
         copy = remote(src, dst, take(1), target)
+        copy.start()
+        sent.append(copy)
+        return copy
+
+    def post_if(src, dst, target, sends, takes, blank=None):
+        copy = Guarded(remote(src, dst, take(1), target), sends, takes, blank)
         copy.start()
         sent.append(copy)
         return copy
@@ -198,13 +235,23 @@
     load_kg.start()
     load_cot.start()
     barrier = pltpu.get_barrier_semaphore()
-    partners = [at_device(device + 1), at_device(device - 1)]
-    partners += [(seq, peer(k)) for k in range(1, MEMBERS)]
-    partners += [at_seq(unit_base + lax.rem(in_unit + k, 4)) for k in range(1, 4)]
-    partners += [at_seq(unit_base + 4 + k) for k in range(4)]
-    partners += [at_seq(unit_base - 4 + k) for k in range(4)]
-    for partner in partners:
-        pl.semaphore_signal(barrier, inc=1, device_id=partner, device_id_type=MESH)
+    partners = [(at_device(device + 1), no(last_device)), (at_device(device - 1), no(first_device))]
+    partners += [((seq, peer(k)), None) for k in range(1, MEMBERS)]
+    partners += [(at_seq(unit_base + lax.rem(in_unit + k, 4)), None) for k in range(1, 4)]
+    partners += [(at_seq(unit_base + 4 + k), no(last_unit)) for k in range(4)]
+    partners += [(at_seq(unit_base - 4 + k), no(first_unit)) for k in range(4)]
+    expected = 0
+    for partner, present in partners:
+
+        def greet(partner=partner):
+            pl.semaphore_signal(barrier, inc=1, device_id=partner, device_id_type=MESH)
+
+        if present is None:
+            greet()
+            expected = expected + 1
+        else:
+            pl.when(present)(greet)
+            expected = expected + jnp.where(present, 1, 0)
 
     load_tok.wait()
 
@@ -217,19 +264,21 @@
         return 0
 
     lax.fori_loop(0, ROWS // 16, normalize_rows, 0)
-    pl.semaphore_wait(barrier, len(partners))
+    pl.semaphore_wait(barrier, expected)
 
     halo_index = take(4)
 
     def halo(chunk):
         here = cols(chunk)
-        return remote(n0.at[:, here], n0p.at[:, here], halo_index + chunk, at_device(device + 1))
+        copy = remote(n0.at[:, here], n0p.at[:, here], halo_index + chunk, at_device(device + 1))
+        return Guarded(copy, no(last_device), no(first_device), n0p.at[:, here])
 
     for chunk in range(4):
         halo(chunk).start()
     load_cot.wait()
-    cot_edge = post(
-        cotx.at[pl.ds(0, 16)], cotx.at[pl.ds(ROWS, 16)], at_device(device - 1)
+    cot_edge = post_if(
+        cotx.at[pl.ds(0, 16)], cotx.at[pl.ds(ROWS, 16)], at_device(device - 1),
+        no(first_device), no(last_device), cotx.at[pl.ds(ROWS, 16)],
     )
 
     load_qg.wait()
@@ -260,11 +309,10 @@
 
     cot_edge.wait_recv()
     row, col = iotas(48, ROWS + 16)
-    known = (col < ROWS) | (device < devices - 1)
     first = (row < 32) & (col >= 4 * row + 3) & (col <= 4 * row + 6)
     start = 16 * (row - 32) + 15
     second = (row >= 32) & (row < 40) & (col >= start) & (col < start + 16)
-    gather = ones_where(known & (first | second))
+    gather = ones_where(first | second)
     for chunk in range(4):
         here = pl.ds(chunk * COLS, COLS)
         summed = dot(gather, cotx[:, here])
@@ -273,7 +321,7 @@
     gm_low[...] = gmr[...].astype(BF16)
 
     arrived(n1_copies)
-    n1_next = post(n1c, n1p, at_seq(seq + 1))
+    n1_next = post_if(n1c, n1p, at_seq(seq + 1), no(last_group), no(first_group), n1p)
     g2_copies = to_members(lambda t: g2r.at[:, cols(t)], g2h.at[rows(sub, 8)])
     gm_copies = to_members(lambda t: gm_low.at[:, cols(t)], gmh.at[rows(sub, 32)])
     g2h[rows(sub, 8), :] = g2r[:, cols(sub)]
@@ -322,7 +370,11 @@
         for k in range(1, 4)
     ]
     n2_copies += [
-        post(n2r.at[:, head_cols(seq_peer(k))], n2p.at[rows(in_unit, 32)], at_seq(unit_base + 4 + seq_peer(k)))
+        post_if(
+            n2r.at[:, head_cols(seq_peer(k))], n2p.at[rows(in_unit, 32)],
+            at_seq(unit_base + 4 + seq_peer(k)),
+            no(last_unit), no(first_unit), n2p if k == 0 else None,
+        )
         for k in range(4)
     ]
     n2c[rows(in_unit, 32), :] = n2r[:, head_cols(in_unit)]
@@ -340,7 +392,10 @@
     c2[:, HEAD : 2 * HEAD] = term_cur.astype(BF16)
     gp2[...] = term_prev.astype(BF16)
     c2_copies = [
-        post(gp2.at[rows(seq_peer(k), 32)], r2p.at[in_unit], at_seq(unit_base - 4 + seq_peer(k)))
+        post_if(
+            gp2.at[rows(seq_peer(k), 32)], r2p.at[in_unit], at_seq(unit_base - 4 + seq_peer(k)),
+            no(first_unit), no(last_unit), r2p if k == 0 else None,
+        )
         for k in range(4)
     ]
     c2_copies += [
@@ -367,7 +422,7 @@
     edge[...] = jnp.where(
         row == 0, u2_wide[31:32], jnp.where(row == 1, u1_row(ROWS - 1), 0.0)
     ).astype(BF16)
-    edge_copy = post(edge, edge_in, at_seq(seq + 1))
+    edge_copy = post_if(edge, edge_in, at_seq(seq + 1), no(last_group), no(first_group), edge_in)
 
     arrived(dz_copies)
     total = unpacked(dz[...] + dz_in[0] + dz_in[1] + dz_in[2])
@@ -388,7 +443,11 @@
     )
     for k, (term_cur, term_prev) in enumerate(results):
         gp1[k] = term_prev.astype(BF16)
-        back_copies.append(post(gp1.at[k], gr1.at[k], at_seq(seq - 1)))
+        back_copies.append(
+            post_if(
+                gp1.at[k], gr1.at[k], at_seq(seq - 1), no(first_group), no(last_group), gr1.at[k]
+            )
+        )
         gc1[:, spans[k]] = term_cur
 
     edge_copy.wait_recv()
@@ -424,7 +483,8 @@
 
     def back_halo(chunk):
         here = cols(chunk)
-        return remote(gp0.at[:, here], gr0.at[:, here], back_index + chunk, at_device(device - 1))
+        copy = remote(gp0.at[:, here], gr0.at[:, here], back_index + chunk, at_device(device - 1))
+        return Guarded(copy, no(first_device), no(last_device), gr0.at[:, here])
 
     def backward_chunk(chunk, _):
         wide = cols(chunk)

time: 91.6 us -> 86 us (0.939)
  the two profiles are of different devices: /device:TPU:64 before, /device:TPU:384 now
where the time goes in v3:
time: 86 us; the launch traced here: 85.7 us
  Pallas kernels  81.9 us (95%)
  local copies, waits for them, and re-layouts  3.1 us (4%)
    pallas_call x1, Pallas kernels, per_device(): pl.pallas_call(body, out_shape=(shape, shape), in_specs=[hbm] * 4, out_sp...  81.9 us
    unnamed x6, local copies, waits for them, and re-layouts  3.1 us

profile of v3, /device:TPU:384, one launch (start us, length us, event | category | flops | bytes accessed | tf_op | source)
XLA Modules:
  0.0 85.7 jit_solution(12436877700503820506)
XLA Ops:
  0.6 0.0 copy-start
  0.6 0.7 copy-done
  1.4 0.0 copy-start.1
  1.4 0.8 copy-done.1
  2.1 81.9 %shard_map.59 = (bf16[128,2048]{1,0:T(8,128)(2,1)S(1)}, bf16[128,2048]{1,0:T(8,128)(2,1)S(1)}) custom-call(bf16[128,2048]{1,0:T(8,128)(2,1)} %refs_0_.1, bf16[128,2048]{1,0:T(8,128)(2,1)} %refs_1_.1, f32[3,2048]{1,0:T(4,128)S(1)} %copy-done, f32[3,2048]{1,0:T(4,128)S(1)} %copy-done.1), custom_call_target="tpu_custom_call" | custom-call | tf_op jit(solution)/shard_map/pallas_call | solution.py:588
  84.1 0.8 copy.8
  84.9 0.8 copy.9
Async XLA Ops:
  0.6 0.8 copy-start
  1.4 0.8 copy-start.1

commit v4 on v3

--- a/solution.py
+++ b/solution.py
@@ -84,7 +84,6 @@
     queries = [gained(h[0], h[2]) for h in heads]
     d_probs = [jnp.where(own, dot_t(h[5], h[0]), dot_t(h[5], h[1])) for h in heads]
     low = [h[4].astype(BF16) for h in heads]
-    v_cur = [t_dot(jnp.where(own, p, zero), h[5]) for p, h in zip(low, heads)]
     v_prev = [t_dot(jnp.where(own, zero, p), h[5]) for p, h in zip(low, heads)]
     centers = [jnp.sum(h[4] * d, axis=-1, keepdims=True) for h, d in zip(heads, d_probs)]
     d_scores = [
@@ -93,15 +92,20 @@
     ds_cur = [jnp.where(own, d, zero) for d in d_scores]
     ds_prev = [jnp.where(own, zero, d) for d in d_scores]
     k_prev = [t_dot(d, q) for d, q in zip(ds_prev, queries)]
-    k_cur = [t_dot(d, q) for d, q in zip(ds_cur, queries)]
-    d_query = [
-        dot(a, gained(h[0], h[3])) + dot(b, gained(h[1], h[3]))
-        for a, b, h in zip(ds_cur, ds_prev, heads)
-    ]
-    return [
-        (dq * h[2] + kc * h[3] + vc, kp * h[3] + vp)
-        for h, dq, kc, vc, kp, vp in zip(heads, d_query, k_cur, v_cur, k_prev, v_prev)
-    ]
+    terms_prev = [kp * h[3] + vp for h, kp, vp in zip(heads, k_prev, v_prev)]
+
+    def own_terms():
+        v_cur = [t_dot(jnp.where(own, p, zero), h[5]) for p, h in zip(low, heads)]
+        k_cur = [t_dot(d, q) for d, q in zip(ds_cur, queries)]
+        d_query = [
+            dot(a, gained(h[0], h[3])) + dot(b, gained(h[1], h[3]))
+            for a, b, h in zip(ds_cur, ds_prev, heads)
+        ]
+        return [
+            dq * h[2] + kc * h[3] + vc for h, dq, kc, vc in zip(heads, d_query, k_cur, v_cur)
+        ]
+
+    return terms_prev, own_terms
 
 
 def packed(column):
@@ -387,9 +391,7 @@
     bias2 = jnp.where(unit_base > 0, 0.0, NEGATIVE_FILL).astype(F32)
     gains2 = gains(2, in_unit)
     ((probs2, attended2),) = forward_heads([(n2c[...], n2p[...], *gains2)], bias2)
-    ((term_cur, term_prev),) = backward_heads([(n2c[...], n2p[...], *gains2, probs2, gl2h[...])])
-    c2[:, 0:HEAD] = attended2.astype(BF16)
-    c2[:, HEAD : 2 * HEAD] = term_cur.astype(BF16)
+    (term_prev,), own_terms2 = backward_heads([(n2c[...], n2p[...], *gains2, probs2, gl2h[...])])
     gp2[...] = term_prev.astype(BF16)
     c2_copies = [
         post_if(
@@ -398,6 +400,8 @@
         )
         for k in range(4)
     ]
+    c2[:, 0:HEAD] = attended2.astype(BF16)
+    c2[:, HEAD : 2 * HEAD] = own_terms2()[0].astype(BF16)
     c2_copies += [
         post(c2.at[rows(seq_peer(k), 32)], r2c.at[in_unit], at_seq(unit_base + seq_peer(k)))
         for k in range(1, 4)
@@ -435,19 +439,20 @@
     grad1 = gmh[...].astype(F32) + split_dot(repeat_matrix(), b2[...]) * 0.25
     gl1[...] = grad1.astype(BF16)
     back_copies = []
-    results = backward_heads(
+    terms_prev, own_terms1 = backward_heads(
         [
             (n1c[:, here], n1p[:, here], *gains(1, k), p1[k], gl1[:, here])
             for k, here in enumerate(spans)
         ]
     )
-    for k, (term_cur, term_prev) in enumerate(results):
+    for k, term_prev in enumerate(terms_prev):
         gp1[k] = term_prev.astype(BF16)
         back_copies.append(
             post_if(
                 gp1.at[k], gr1.at[k], at_seq(seq - 1), no(first_group), no(last_group), gr1.at[k]
             )
         )
+    for k, term_cur in enumerate(own_terms1()):
         gc1[:, spans[k]] = term_cur
 
     edge_copy.wait_recv()
@@ -492,17 +497,17 @@
         g0[:, wide] = grad
         spans = [pl.ds(multiple(chunk * COLS + k * HEAD, HEAD), HEAD) for k in range(4)]
         low = grad.astype(BF16)
-        results = backward_heads(
+        terms_prev, own_terms0 = backward_heads(
             [
                 (n0[:, here], n0p[:, here], qg[0:1, here], kg[0:1, here],
                  p0[chunk * 4 + k], low[:, k * HEAD : (k + 1) * HEAD])
                 for k, here in enumerate(spans)
             ]
         )
-        for here, (_, term_prev) in zip(spans, results):
+        for here, term_prev in zip(spans, terms_prev):
             gp0[:, here] = term_prev.astype(BF16)
         back_halo(chunk).start()
-        for here, (term_cur, _) in zip(spans, results):
+        for here, term_cur in zip(spans, own_terms0()):
             gc0[:, here] = term_cur
         return 0
 

time: 86 us -> 85.6 us (level)
  no operation moved by 1% of the time
where the time goes in v4:
time: 85.6 us; the launch traced here: 85.4 us
  Pallas kernels  81.6 us (95%)
  local copies, waits for them, and re-layouts  3.1 us (4%)
    pallas_call x1, Pallas kernels, per_device(): pl.pallas_call(body, out_shape=(shape, shape), in_specs=[hbm] * 4, out_sp...  81.6 us
    unnamed x6, local copies, waits for them, and re-layouts  3.1 us

profile of v4, /device:TPU:384, one launch (start us, length us, event | category | flops | bytes accessed | tf_op | source)
XLA Modules:
  0.0 85.4 jit_solution(10298156487140733496)
XLA Ops:
  0.6 0.0 copy-start
  0.6 0.7 copy-done
  1.4 0.0 copy-start.1
  1.4 0.8 copy-done.1
  2.1 81.6 %shard_map.59 = (bf16[128,2048]{1,0:T(8,128)(2,1)S(1)}, bf16[128,2048]{1,0:T(8,128)(2,1)S(1)}) custom-call(bf16[128,2048]{1,0:T(8,128)(2,1)} %refs_0_.1, bf16[128,2048]{1,0:T(8,128)(2,1)} %refs_1_.1, f32[3,2048]{1,0:T(4,128)S(1)} %copy-done, f32[3,2048]{1,0:T(4,128)S(1)} %copy-done.1), custom_call_target="tpu_custom_call" | custom-call | tf_op jit(solution)/shard_map/pallas_call | solution.py:593
  83.8 0.8 copy.8
  84.6 0.8 copy.9
Async XLA Ops:
  0.6 0.8 copy-start
  1.4 0.8 copy-start.1

commit v5 on v4

--- a/solution.py
+++ b/solution.py
@@ -327,7 +327,6 @@
     arrived(n1_copies)
     n1_next = post_if(n1c, n1p, at_seq(seq + 1), no(last_group), no(first_group), n1p)
     g2_copies = to_members(lambda t: g2r.at[:, cols(t)], g2h.at[rows(sub, 8)])
-    gm_copies = to_members(lambda t: gm_low.at[:, cols(t)], gmh.at[rows(sub, 32)])
     g2h[rows(sub, 8), :] = g2r[:, cols(sub)]
     gmh[rows(sub, 32), :] = gm_low[:, cols(sub)]
 
@@ -383,6 +382,7 @@
     ]
     n2c[rows(in_unit, 32), :] = n2r[:, head_cols(in_unit)]
 
+    gm_copies = to_members(lambda t: gm_low.at[:, cols(t)], gmh.at[rows(sub, 32)])
     u1_copies = to_members(lambda t: u1.at[rows(t, 32)], u1r.at[:, cols(sub)])
     u1r[:, cols(sub)] = u1[rows(sub, 32), :]
 

time: 85.6 us -> 84.5 us (0.987)
  Pallas kernels: 81.6 us -> 80.5 us
    pallas_call x1, Pallas kernels: 81.6 us -> 80.5 us  [per_device(): pl.pallas_call(body, out_shape=(shape, shape), in_specs=[hbm] * 4, out_sp...]
where the time goes in v5:
time: 84.5 us; the launch traced here: 84.2 us
  Pallas kernels  80.5 us (95%)
  local copies, waits for them, and re-layouts  3.1 us (4%)
    pallas_call x1, Pallas kernels, per_device(): pl.pallas_call(body, out_shape=(shape, shape), in_specs=[hbm] * 4, out_sp...  80.5 us
    unnamed x6, local copies, waits for them, and re-layouts  3.1 us

profile of v5, /device:TPU:384, one launch (start us, length us, event | category | flops | bytes accessed | tf_op | source)
XLA Modules:
  0.0 84.2 jit_solution(13542426724390093126)
XLA Ops:
  0.6 0.0 copy-start
  0.6 0.7 copy-done
  1.4 0.0 copy-start.1
  1.4 0.8 copy-done.1
  2.1 80.5 %shard_map.59 = (bf16[128,2048]{1,0:T(8,128)(2,1)S(1)}, bf16[128,2048]{1,0:T(8,128)(2,1)S(1)}) custom-call(bf16[128,2048]{1,0:T(8,128)(2,1)} %refs_0_.1, bf16[128,2048]{1,0:T(8,128)(2,1)} %refs_1_.1, f32[3,2048]{1,0:T(4,128)S(1)} %copy-done, f32[3,2048]{1,0:T(4,128)S(1)} %copy-done.1), custom_call_target="tpu_custom_call" | custom-call | tf_op jit(solution)/shard_map/pallas_call | solution.py:593
  82.6 0.8 copy.8
  83.4 0.8 copy.9
Async XLA Ops:
  0.6 0.8 copy-start
  1.4 0.8 copy-start.1
